TPU v7x, 512 devices: a whole 4x8x8 slice. The times are simulated.
512 devices in a mesh: blk: 16 (over y, core), bal: 32 (over x, z).
Axes of the slice: x: 4, y: 8, z: 8, core: 2. Of those that a mesh axis runs over, the one named last changes fastest.
Arguments:
- flow_state: float32 [64, 1024, 6, 128], P('blk', 'bal'), may hold values from -6 to 6
- source: float32 [64, 1024, 6, 128], P('blk', 'bal'), may hold values from -6 to 6
- diag_scale: float32 [64, 1024, 128], P('blk', 'bal'), may hold values from 1.5 to 6
- flux_jac: float32 [4, 6, 6], replicated, may hold values from -0.875 to 0.875
- line_coupling: float32 [2, 6, 6], replicated, may hold values from -0.625 to 0.625
- block_inverse: float32 [6, 6], replicated, may hold values from -0.15 to 1.2, as said below
- active_order: int32 [16, 32, 128], P('blk', 'bal'), may hold values from 0 to 127, each once within a row
- active_units: int32 [16, 32], P('blk', 'bal'), may hold values from 1 to 3, 64 in all within a row
- donor_cells: int32 [16, 32, 8, 16, 128], P('blk', 'bal'), may hold values from 0 to 16383
- donor_weights: float32 [16, 32, 8, 16, 128], P('blk', 'bal'), may hold values from 0.1 to 1
- receptor_cells: int32 [16, 32, 16, 128], P('blk', 'bal'), may hold values from 0 to 16383, as said below
Outputs:
- updated: float32 [64, 1024, 6, 128], P('blk', 'bal')
Inputs may be any that keep to these rules, and one draw needn't show every extreme that they name: `active_order`: each grid block's list holds every local line index once. `active_units`: over the grid blocks of one row along the second dimension the units sum to exactly 64, and one of them holds 3. `donor_cells`: local cell indices within the donor's grid block. `receptor_cells`: local cell indices within the receptor's grid block, all distinct within one grid block. `block_inverse`: diagonally dominant.
All inputs are finite; a program needn't handle non-finite values.
Results may differ from a plain program's by a relative error of at most 0.0003.
Values sent between devices are 32-bit elements; how exact they have to be, the bound alone decides.
No kernel may reach another device: no remote copies, remote signals or barrier semaphores. Data moves between devices by JAX's collectives and lax.ppermute only.
A program may use at most 64 MiB of HBM per device.

v0:
```python
import jax
import jax.numpy as jnp
from jax import lax
from jax.sharding import PartitionSpec as P

SWEEPS = 4


def with_halo(cells, sides, width):
    for axis, dim in sides:
        count = lax.axis_size(axis)
        ends = count - 1
        head = lax.slice_in_dim(cells, 0, width, axis=dim)
        tail = lax.slice_in_dim(cells, cells.shape[dim] - width, cells.shape[dim], axis=dim)
        cells = jnp.concatenate(
            [
                lax.ppermute(tail, axis, [(i, (i + 1) % count) for i in range(ends)]),
                cells,
                lax.ppermute(head, axis, [((i + 1) % count, i) for i in range(ends)]),
            ],
            axis=dim,
        )
    return cells


def apply_block(matrix, values):
    return jnp.einsum("fg,...gp->...fp", matrix, values, precision=lax.Precision.HIGHEST)


def sweep_rows(residual, scales, coupling, inverse):
    correction = jnp.zeros_like(residual)
    for number in range(SWEEPS):
        zero_edge = jnp.zeros_like(correction[..., :1])
        below_cells = jnp.concatenate([zero_edge, correction[..., :-1]], axis=-1)
        above_cells = jnp.concatenate([correction[..., 1:], zero_edge], axis=-1)
        inner = (
            residual - apply_block(coupling[0], below_cells) - apply_block(coupling[1], above_cells)
        )
        correction = apply_block(inverse, inner) / scales[..., None, :]
    return correction


def interpolate(block_rows, cell_list, weights):
    fields = block_rows.shape[1]
    length = block_rows.shape[2]
    field_index = jnp.arange(fields, dtype=jnp.int32).reshape(fields, 1, 1, 1)
    picked = block_rows[(cell_list // length)[None], field_index, (cell_list % length)[None]]
    shares = weights / jnp.sum(weights, axis=0, keepdims=True)
    return jnp.sum(shares[None] * picked, axis=1)


def place(block_rows, cell_list, incoming):
    fields = block_rows.shape[1]
    length = block_rows.shape[2]
    field_index = jnp.arange(fields, dtype=jnp.int32).reshape(fields, 1, 1)
    return block_rows.at[(cell_list // length)[None], field_index, (cell_list % length)[None]].set(
        incoming
    )


def shards(
    flow_state,
    source,
    diag_scale,
    flux_jac,
    line_coupling,
    block_inverse,
    active_order,
    active_units,
    donor_cells,
    donor_weights,
    receptor_cells,
):
    width_x, width_y, fields, length = flow_state.shape
    rows_dev = width_x * width_y
    peer_count = lax.axis_size("bal")
    unit_rows = rows_dev // (4 * peer_count)
    slot_count = 3 * unit_rows
    padded = with_halo(flow_state, (("blk", 0), ("bal", 1)), 1)
    flux_sum = apply_block(flux_jac[0], flow_state - padded[:-2, 1:-1])
    flux_sum = flux_sum + apply_block(flux_jac[1], flow_state - padded[2:, 1:-1])
    flux_sum = flux_sum + apply_block(flux_jac[2], flow_state - padded[1:-1, :-2])
    flux_sum = flux_sum + apply_block(flux_jac[3], flow_state - padded[1:-1, 2:])
    residual = (source - flux_sum).reshape(rows_dev, fields, length)
    scale_rows = diag_scale.reshape(rows_dev, length)
    ordering = active_order.reshape(rows_dev)
    unit_count = active_units.reshape(())
    slot_rows = jnp.transpose(ordering[: peer_count * slot_count].reshape(slot_count, peer_count))
    slot_used = (
        jnp.arange(slot_count, dtype=jnp.int32).reshape(1, slot_count) < unit_count * unit_rows
    )
    send_rows = jnp.where(slot_used[:, :, None, None], residual[slot_rows], 0.0)
    send_scales = jnp.where(slot_used[:, :, None], scale_rows[slot_rows], 1.0)
    counts = jnp.full((peer_count, 1), unit_count, jnp.int32)
    rows_in, scales_in, counts_in = (
        lax.all_to_all(send_rows, "bal", split_axis=0, concat_axis=0, tiled=True),
        lax.all_to_all(send_scales, "bal", split_axis=0, concat_axis=0, tiled=True),
        lax.all_to_all(counts, "bal", split_axis=0, concat_axis=0, tiled=True),
    )
    counts_rows = counts_in.reshape(peer_count) * unit_rows
    starts = jnp.cumsum(counts_rows) - counts_rows
    filled = 2 * peer_count * unit_rows
    position = jnp.arange(filled, dtype=jnp.int32)
    source_peer = (
        jnp.sum(
            (starts.reshape(1, peer_count) <= position.reshape(filled, 1)).astype(jnp.int32), axis=1
        )
        - 1
    )
    flat_slot = source_peer * slot_count + position - starts[source_peer]
    packed = rows_in.reshape(peer_count * slot_count, fields, length)[flat_slot]
    packed_scales = scales_in.reshape(peer_count * slot_count, length)[flat_slot]
    solved = sweep_rows(packed, packed_scales, line_coupling, block_inverse)
    slot_index = starts.reshape(peer_count, 1) + jnp.arange(slot_count, dtype=jnp.int32).reshape(
        1, slot_count
    )
    slot_live = jnp.arange(slot_count, dtype=jnp.int32).reshape(
        1, slot_count
    ) < counts_rows.reshape(peer_count, 1)
    returning = jnp.where(
        slot_live[:, :, None, None], solved[jnp.minimum(slot_index, filled - 1)], 0.0
    )
    returned = lax.all_to_all(returning, "bal", split_axis=0, concat_axis=0, tiled=True)
    correction = (
        jnp.zeros_like(residual)
        .at[slot_rows.reshape(peer_count * slot_count)]
        .set(returned.reshape(peer_count * slot_count, fields, length))
    )
    corrected = flow_state.reshape(rows_dev, fields, length) + correction
    values = interpolate(
        corrected,
        donor_cells.reshape(donor_cells.shape[2:]),
        donor_weights.reshape(donor_weights.shape[2:]),
    )
    incoming = lax.all_to_all(values, "blk", split_axis=1, concat_axis=1, tiled=True)
    updated = place(corrected, receptor_cells.reshape(receptor_cells.shape[2:]), incoming)
    return updated.reshape(width_x, width_y, fields, length)


def solution(mesh):
    placed = (
        P("blk", "bal", None, None),
        P("blk", "bal", None, None),
        P("blk", "bal", None),
        P(),
        P(),
        P(),
        P("blk", "bal", None),
        P("blk", "bal"),
        P("blk", "bal", None, None, None),
        P("blk", "bal", None, None, None),
        P("blk", "bal", None, None),
    )
    return jax.shard_map(
        shards, mesh=mesh, in_specs=placed, out_specs=P("blk", "bal", None, None), check_vma=False
    )
```

profile of v0, /device:TPU:7, one launch (start us, length us, event | category | flops | bytes accessed | tf_op | source)
XLA Modules:
  0.0 737.8 jit_solution(18168362980953523017)
XLA Ops:
  0.0 1.0 fusion.64
  1.0 3.8 collective-permute-start
  4.8 1.9 collective-permute-start.1
  8.0 12.9 %all-to-all-start = ((s32[32,1,1]{2,1,0:T(1,128)}), s32[32,1,1]{2,1,0:T(1,128)S(1)}, u32[]{:S(2)}, u32[]{:S(2)}) async-start(s32[32,1,1]{2,1,0:T(1,128)} %broadcast_in_dim.53), calls=%async_computation | async-start | bytes 32768 | tf_op jit(solution)/shard_map/all_to_all | solution.py:98
  20.9 0.9 fusion.68
  25.4 2.5 all-to-all-done
  27.8 6.8 all-to-all-start.2
  35.8 3.1 collective-permute-start.2
  38.9 4.3 collective-permute-start.3
  44.2 0.8 fusion.16
  45.0 0.8 convolution_add_fusion.2
  45.8 0.8 convolution_add_fusion.1
  46.8 1.0 fusion.1
  48.5 0.8 broadcast_select_fusion.1
  49.4 9.1 %all-to-all-start.1 = ((f32[32,3,6,128]{3,2,1,0:T(8,128)}), f32[32,3,6,128]{3,2,1,0:T(8,128)S(1)}, u32[]{:S(2)}, u32[]{:S(2)}) async-start(f32[32,3,6,128]{3,2,1,0:T(8,128)} %broadcast_select_fusion.1), calls=%async_computation.1 | async-start | bytes 786432 | tf_op jit(solution)/shard_map/all_to_all | solution.py:96
  60.0 9.6 %all-to-all-done.1 = f32[32,3,6,128]{3,2,1,0:T(8,128)S(1)} async-done(((f32[32,3,6,128]{3,2,1,0:T(8,128)}), f32[32,3,6,128]{3,2,1,0:T(8,128)S(1)}, u32[]{:S(2)}, u32[]{:S(2)}) %all-to-all-start.1) | async-done | bytes 294944 | tf_op jit(solution)/shard_map/all_to_all | solution.py:96
  75.9 0.9 broadcast_select_fusion
  76.9 8.4 %all-to-all-start.3 = ((f32[32,3,6,128]{3,2,1,0:T(8,128)}), f32[32,3,6,128]{3,2,1,0:T(8,128)S(1)}, u32[]{:S(2)}, u32[]{:S(2)}) async-start(f32[32,3,6,128]{3,2,1,0:T(8,128)} %broadcast_select_fusion), calls=%async_computation.3 | async-start | bytes 786432 | tf_op jit(solution)/shard_map/all_to_all | solution.py:123
  85.5 10.2 %all-to-all-done.3 = f32[32,3,6,128]{3,2,1,0:T(8,128)S(1)} async-done(((f32[32,3,6,128]{3,2,1,0:T(8,128)}), f32[32,3,6,128]{3,2,1,0:T(8,128)S(1)}, u32[]{:S(2)}, u32[]{:S(2)}) %all-to-all-start.3) | async-done | bytes 294944 | tf_op jit(solution)/shard_map/all_to_all | solution.py:123
  95.7 3.4 scatter_fusion
  99.3 574.9 %gather_fusion.6 = f32[98304]{0:T(1024)S(1)} fusion(f32[128,6,128]{2,1,0:T(8,128)S(1)} %copy_add_fusion, s32[98304]{0:T(1024)S(1)} %bitcast.202), kind=kCustom, calls=%fused_computation.6 | custom fusion | bytes 1966080 | tf_op jit(solution)/shard_map/gather | solution.py:47
  674.9 8.7 %all-to-all-start.4 = ((f32[6,16,128]{2,0,1:T(8,128)}), f32[6,16,128]{2,0,1:T(8,128)S(1)}, u32[]{:S(2)}, u32[]{:S(2)}) async-start(f32[6,16,128]{2,0,1:T(8,128)} %copy.98), calls=%async_computation.4 | async-start | bytes 131072 | tf_op jit(solution)/shard_map/all_to_all | solution.py:135
  683.7 7.7 %all-to-all-done.4 = f32[6,16,128]{2,0,1:T(8,128)S(1)} async-done(((f32[6,16,128]{2,0,1:T(8,128)}), f32[6,16,128]{2,0,1:T(8,128)S(1)}, u32[]{:S(2)}, u32[]{:S(2)}) %all-to-all-start.4) | async-done | bytes 49184 | tf_op jit(solution)/shard_map/all_to_all | solution.py:135
  691.5 45.6 %scatter_fusion.1 = f32[98304]{0:T(1024)S(1)} fusion(f32[98304]{0:T(1024)S(1)} %bitcast.200, s32[12288]{0:T(1024)S(1)} %bitcast.210, f32[12288]{0:T(1024)S(1)} %bitcast.211), kind=kCustom, calls=%fused_computation.8 | custom fusion | bytes 196608
  (95 shorter events, 16.8 us)
Async XLA Ops:
  0.0 23.5 %copy-start = (f32[4,32,128]{2,1,0:T(8,128)S(1)}, f32[4,32,128]{2,1,0:T(8,128)}, u32[]{:S(2)}) copy-start(f32[4,32,128]{2,1,0:T(8,128)} %param.13) | copy-start | bytes 196612
  0.0 24.4 %copy-start.3 = (f32[1,1,8,16,128]{4,3,2,1,0:T(8,128)S(1)}, f32[1,1,8,16,128]{4,3,2,1,0:T(8,128)}, u32[]{:S(2)}) copy-start(f32[1,1,8,16,128]{4,3,2,1,0:T(8,128)} %param.20) | copy-start | bytes 196612
  1.0 23.5 %copy-start.5 = (s32[1,1,16,128]{3,2,1,0:T(8,128)S(1)}, s32[1,1,16,128]{3,2,1,0:T(8,128)}, u32[]{:S(2)}) copy-start(s32[1,1,16,128]{3,2,1,0:T(8,128)} %param.21) | copy-start | bytes 24580
  1.0 34.6 %collective-permute-start = (f32[1,32,6,128]{3,1,2,0:T(8,128)S(1)}, f32[1,32,6,128]{3,1,2,0:T(8,128)S(1)}, u32[]{:S(2)}, u32[]{:S(2)}) collective-permute-start(f32[1,32,6,128]{3,1,2,0:T(8,128)S(1)} %get-tuple-element.11), channel_id=1, source_target_pairs={{0,32},{32,64},{64,96},{96,128},{128,160},{160,192},{192,224},{224... | collective-permute-start | bytes 294920 | tf_op jit(solution)/shard_map/ppermute | solution.py:17
  4.8 30.9 %collective-permute-start.1 = (f32[1,32,6,128]{3,1,2,0:T(8,128)S(1)}, f32[1,32,6,128]{3,1,2,0:T(8,128)S(1)}, u32[]{:S(2)}, u32[]{:S(2)}) collective-permute-start(f32[1,32,6,128]{3,1,2,0:T(8,128)S(1)} %get-tuple-element.12), channel_id=1, source_target_pairs={{32,0},{64,32},{96,64},{128,96},{160,128},{192,160},{224,192},{256... | collective-permute-start | bytes 294920 | tf_op jit(solution)/shard_map/ppermute | solution.py:19
  8.0 19.9 %all-to-all-start = ((s32[32,1,1]{2,1,0:T(1,128)}), s32[32,1,1]{2,1,0:T(1,128)S(1)}, u32[]{:S(2)}, u32[]{:S(2)}) async-start(s32[32,1,1]{2,1,0:T(1,128)} %broadcast_in_dim.53), calls=%async_computation | async-start | bytes 32768 | tf_op jit(solution)/shard_map/all_to_all | solution.py:98
  23.5 1.7 copy-start.7
  23.5 1.8 copy-start.1
  27.8 21.5 %all-to-all-start.2 = ((f32[32,3,128]{2,1,0:T(4,128)}), f32[32,3,128]{2,1,0:T(4,128)S(1)}, u32[]{:S(2)}, u32[]{:S(2)}) async-start(f32[32,3,128]{2,1,0:T(4,128)} %broadcast_select_fusion.2), calls=%async_computation.2 | async-start | bytes 131072 | tf_op jit(solution)/shard_map/all_to_all | solution.py:97
  35.8 7.5 %collective-permute-start.2 = (f32[6,1,6,128]{3,1,2,0:T(1,128)S(1)}, f32[6,1,6,128]{3,1,2,0:T(1,128)S(1)}, u32[]{:S(2)}, u32[]{:S(2)}) collective-permute-start(f32[6,1,6,128]{3,1,2,0:T(1,128)S(1)} %get-tuple-element.8), channel_id=1, source_target_pairs={{0,1},{1,2},{2,3},{3,4},{4,5},{5,6},{6,7},{7,8},{8,9},{9,10},{10,1... | collective-permute-start | bytes 55304 | tf_op jit(solution)/shard_map/ppermute | solution.py:17
  38.9 5.2 collective-permute-start.3
  45.8 1.0 copy-start.2
  49.4 20.2 %all-to-all-start.1 = ((f32[32,3,6,128]{3,2,1,0:T(8,128)}), f32[32,3,6,128]{3,2,1,0:T(8,128)S(1)}, u32[]{:S(2)}, u32[]{:S(2)}) async-start(f32[32,3,6,128]{3,2,1,0:T(8,128)} %broadcast_select_fusion.1), calls=%async_computation.1 | async-start | bytes 786432 | tf_op jit(solution)/shard_map/all_to_all | solution.py:96
  70.3 0.7 copy-start.8
  76.8 8.4 %copy-start.6 = (s32[3]{0:T(128)S(1)}, s32[3]{0:T(128)}, u32[]{:S(2)}) copy-start(s32[3]{0:T(128)} %constant.104) | copy-start | bytes 40
  76.9 8.5 %copy-start.4 = (s32[1,1,8,16,128]{4,3,2,1,0:T(8,128)S(1)}, s32[1,1,8,16,128]{4,3,2,1,0:T(8,128)}, u32[]{:S(2)}) copy-start(s32[1,1,8,16,128]{4,3,2,1,0:T(8,128)} %param.19) | copy-start | bytes 196612
  76.9 18.8 %all-to-all-start.3 = ((f32[32,3,6,128]{3,2,1,0:T(8,128)}), f32[32,3,6,128]{3,2,1,0:T(8,128)S(1)}, u32[]{:S(2)}, u32[]{:S(2)}) async-start(f32[32,3,6,128]{3,2,1,0:T(8,128)} %broadcast_select_fusion), calls=%async_computation.3 | async-start | bytes 786432 | tf_op jit(solution)/shard_map/all_to_all | solution.py:123
  674.9 16.5 %all-to-all-start.4 = ((f32[6,16,128]{2,0,1:T(8,128)}), f32[6,16,128]{2,0,1:T(8,128)S(1)}, u32[]{:S(2)}, u32[]{:S(2)}) async-start(f32[6,16,128]{2,0,1:T(8,128)} %copy.98), calls=%async_computation.4 | async-start | bytes 131072 | tf_op jit(solution)/shard_map/all_to_all | solution.py:135
where the time goes:
time: 741 us; the launch traced here: 738 us
  local copies, waits for them, and re-layouts  635 us (86%)
  starting transfers between devices  59 us (8%)
  waiting for transfers between devices  30.7 us (4%)
  matrix products  7.83 us (1%)
    gather x1, local copies, waits for them, and re-layouts, interpolate(): block_rows[(cell_list // length)[None], field_index, (cell_list % length)...  575 us
    unnamed x23, local copies, waits for them, and re-layouts  46 us
  transfers between devices with their start and end apart: 9, of which 5 were waited for; matrix products, arithmetic and copies ran while one was open for 2% of the time, Pallas kernels for 0%

commit v1 on v0

v1 whole, which is shorter than its diff:
```python
import functools

import jax
import jax.numpy as jnp
from jax import lax
from jax.experimental import pallas as pl
from jax.experimental.pallas import tpu as pltpu
from jax.sharding import PartitionSpec as P

SWEEPS = 4
FIELDS = 6
DONORS = 8
LANES = 128
INNER = 64
RIM = 72
NOWHERE = 255


def block_product(inverse, coupling, side):
    return [
        [
            sum(inverse[f, h] * coupling[h, side, g] for h in range(FIELDS))
            for g in range(FIELDS)
        ]
        for f in range(FIELDS)
    ]


def apply(matrix, values):
    out = []
    for f in range(FIELDS):
        total = matrix(f, 0) * values[0]
        for g in range(1, FIELDS):
            total = total + matrix(f, g) * values[g]
        out.append(total)
    return out


def solve(residual, scale_inv, inverse, below, above):
    lane = lax.broadcasted_iota(jnp.int32, residual[0].shape, 1)
    first, last = lane == 0, lane == LANES - 1
    base = apply(lambda f, g: inverse[f, g], residual)
    base = [value * scale_inv for value in base]
    correction = base
    for _ in range(SWEEPS - 1):
        total = [None] * FIELDS
        for g in range(FIELDS):
            down = jnp.where(first, 0.0, pltpu.roll(correction[g], 1, 1))
            up = jnp.where(last, 0.0, pltpu.roll(correction[g], LANES - 1, 1))
            for f in range(FIELDS):
                term = below[f][g] * down + above[f][g] * up
                total[f] = term if g == 0 else total[f] + term
        correction = [base[f] - scale_inv * total[f] for f in range(FIELDS)]
    return correction


def fill_table(table, rows, field, first, values):
    high = values.astype(jnp.bfloat16)
    low = (values - high.astype(jnp.float32)).astype(jnp.bfloat16)
    count = values.shape[0]
    table[field * rows + first : field * rows + first + count, 0:LANES] = high
    table[field * rows + first : field * rows + first + count, LANES : 2 * LANES] = low


def gather(table, rows, cells, shares, number):
    at_cell = lax.broadcasted_iota(jnp.int32, (LANES, 2 * LANES), 0)
    at_line = lax.broadcasted_iota(jnp.int32, (rows, 2 * LANES), 0)
    total = [None] * FIELDS
    for k in range(0, DONORS, 2):
        cell = jnp.concatenate([cells[k + i, pl.ds(number, 1), :] for i in (0, 1)], axis=1)
        share = jnp.concatenate([shares[k + i, pl.ds(number, 1), :] for i in (0, 1)], axis=1)
        pick = jnp.where(at_cell == (cell & (LANES - 1)), 1.0, 0.0).astype(jnp.bfloat16)
        found = jnp.dot(
            table[...], jnp.concatenate([pick, pick], axis=0), preferred_element_type=jnp.float32
        )
        weight = jnp.where(at_line == (cell >> 7), share, 0.0)
        for f in range(FIELDS):
            part = found[f * rows : (f + 1) * rows] * weight
            part = jnp.sum(part.reshape(rows // 8, 8, 2 * LANES), axis=0)
            total[f] = part if k == 0 else total[f] + part
    return [
        jnp.sum(value[:, :LANES] + value[:, LANES:], axis=0, keepdims=True) for value in total
    ]


def edges_kernel(flow, x_head, x_tail, y_head, y_tail):
    width_x, _, width_y, _ = flow.shape
    x_head[...] = flow[0]
    x_tail[...] = flow[width_x - 1]
    for f in range(FIELDS):
        for x in range(width_x):
            y_head[f, x : x + 1] = flow[x, f, 0:1]
            y_tail[f, x : x + 1] = flow[x, f, width_y - 1 : width_y]


def inner_kernel(
    jac, coupling, inverse, units, flow, source, diag, order, cells, weights,
    values, near, rim_residual, rim_scale, rim_live, rim_flow, rim_cells, shares,
    live, inner_cells, table,
):
    width_y = flow.shape[2]
    blocks = cells.shape[1]
    line = lax.broadcasted_iota(jnp.int32, (LANES, LANES), 0)
    place = lax.broadcasted_iota(jnp.int32, (LANES, LANES), 1)
    hit = (line == order[...]) & (place < units[0, 0] * 32)
    live[...] = jnp.broadcast_to(
        jnp.max(jnp.where(hit, 1.0, 0.0), axis=1, keepdims=True), (LANES, LANES)
    )
    sums = [
        [jac[f, 0, g] + jac[f, 1, g] + jac[f, 2, g] + jac[f, 3, g] for g in range(FIELDS)]
        for f in range(FIELDS)
    ]
    below = block_product(inverse, coupling, 0)
    above = block_product(inverse, coupling, 1)
    row = lax.broadcasted_iota(jnp.int32, (width_y, LANES), 0)

    cell = cells[...]
    at = cell >> 7
    x, y = at >> 5, at & 31
    middle = (x == 1) | (x == 2)
    edge = middle & ((y == 0) | (y == width_y - 1))
    pos = cell & (LANES - 1)
    inner_cells[...] = (jnp.where(middle & ~edge, at - 32, NOWHERE) << 7) + pos
    on_edge = 64 + (x - 1) + jnp.where(y == 0, 0, 2)
    on_rim = jnp.where(x == 0, at, jnp.where(x == 3, at - 64, NOWHERE))
    rim_cells[...] = (jnp.where(edge, on_edge, on_rim) << 7) + pos
    weight = weights[...]
    shares[...] = weight / jnp.sum(weight, axis=0, keepdims=True)

    def residual_of(plane):
        total = [source[plane, f] for f in range(FIELDS)]
        for g in range(FIELDS):
            here = flow[plane, g]
            left = flow[plane - 1, g] if plane > 0 else None
            right = flow[plane + 1, g] if plane < 3 else None
            before = jnp.where(row == 0, 0.0, pltpu.roll(here, 1, 0))
            after = jnp.where(row == width_y - 1, 0.0, pltpu.roll(here, width_y - 1, 0))
            for f in range(FIELDS):
                value = total[f] - sums[f][g] * here
                if left is not None:
                    value = value + jac[f, 0, g] * left
                if right is not None:
                    value = value + jac[f, 1, g] * right
                total[f] = value + jac[f, 2, g] * before + jac[f, 3, g] * after
        return total

    for number, plane in enumerate((0, 3)):
        residual = residual_of(plane)
        rows = slice(number * width_y, (number + 1) * width_y)
        for f in range(FIELDS):
            rim_residual[f, rows] = residual[f]
            rim_flow[f, rows] = flow[plane, f]
        rim_scale[rows] = 1.0 / diag[plane]
        rim_live[rows] = live[plane * width_y : (plane + 1) * width_y]
    rim_scale[RIM - 8 : RIM] = jnp.ones((8, LANES), jnp.float32)
    rim_live[RIM - 8 : RIM] = jnp.zeros((8, LANES), jnp.float32)
    for f in range(FIELDS):
        rim_residual[f, RIM - 8 : RIM] = jnp.zeros((8, LANES), jnp.float32)
        rim_flow[f, RIM - 8 : RIM] = jnp.zeros((8, LANES), jnp.float32)
    for number, plane in enumerate((1, 2)):
        residual = residual_of(plane)
        scale = 1.0 / diag[plane]
        alive = live[plane * width_y : (plane + 1) * width_y]
        for at_row, y_line in ((64 + number, 0), (66 + number, width_y - 1)):
            for f in range(FIELDS):
                rim_residual[f, at_row : at_row + 1] = residual[f][y_line : y_line + 1]
                rim_flow[f, at_row : at_row + 1] = flow[plane, f, y_line : y_line + 1]
            rim_scale[at_row : at_row + 1] = scale[y_line : y_line + 1]
            rim_live[at_row : at_row + 1] = alive[y_line : y_line + 1]
        correction = solve(residual, scale, inverse, below, above)
        for f in range(FIELDS):
            corrected = flow[plane, f] + jnp.where(alive > 0.5, correction[f], 0.0)
            near[number, f] = corrected
            fill_table(table, INNER, f, number * width_y, corrected)

    @pl.loop(0, blocks)
    def _(number):
        found = gather(table, INNER, inner_cells, shares, number)
        for f in range(FIELDS):
            values[number, f : f + 1, :] = found[f]


def rim_kernel(
    jac, coupling, inverse, x_prev, x_next, y_prev, y_next,
    part, rim_residual, rim_scale, rim_live, rim_flow, rim_cells, shares,
    values, rim, residual, table,
):
    width_y = x_prev.shape[1]
    blocks = rim_cells.shape[1]
    below = block_product(inverse, coupling, 0)
    above = block_product(inverse, coupling, 1)
    for number, (side, halo) in enumerate(((0, x_prev), (1, x_next))):
        rows = slice(number * width_y, (number + 1) * width_y)
        added = apply(lambda f, g: jac[f, side, g], [halo[g] for g in range(FIELDS)])
        for f in range(FIELDS):
            residual[f, rows] = rim_residual[f, rows] + added[f]
    for number, (side, halo) in enumerate(((2, y_prev), (3, y_next))):
        added = apply(lambda f, g: jac[f, side, g], [halo[g] for g in range(FIELDS)])
        for f in range(FIELDS):
            at_row = 64 + 2 * number
            residual[f, at_row : at_row + 2] = (
                rim_residual[f, at_row : at_row + 2] + added[f][1:3]
            )
            for at_row, x in ((number * (width_y - 1), 0), (width_y + number * (width_y - 1), 3)):
                residual[f, at_row : at_row + 1] = (
                    residual[f, at_row : at_row + 1] + added[f][x : x + 1]
                )
    for f in range(FIELDS):
        residual[f, RIM - 4 : RIM] = jnp.zeros((4, LANES), jnp.float32)
    for first in range(0, RIM, 24):
        rows = slice(first, first + 24)
        correction = solve(
            [residual[f, rows] for f in range(FIELDS)], rim_scale[rows], inverse, below, above
        )
        alive = rim_live[rows] > 0.5
        for f in range(FIELDS):
            corrected = rim_flow[f, rows] + jnp.where(alive, correction[f], 0.0)
            rim[f, rows] = corrected
            fill_table(table, RIM, f, first, corrected)

    @pl.loop(0, blocks)
    def _(number):
        found = gather(table, RIM, rim_cells, shares, number)
        for f in range(FIELDS):
            values[number, f : f + 1, :] = found[f] + part[number, f : f + 1, :]


def place_kernel(incoming, receptor, near, rim, updated, spread, pick):
    blocks = incoming.shape[0]
    width_y = near.shape[2]
    count = blocks * LANES
    at_line = lax.broadcasted_iota(jnp.int32, (INNER, LANES), 0)
    at_cell = lax.broadcasted_iota(jnp.int32, (2 * LANES, LANES), 0)
    for number in range(blocks):
        cell = receptor[number : number + 1, :]
        line = cell >> 7
        where = ((line >> 6) << 7) + (cell & (LANES - 1))
        columns = slice(number * LANES, (number + 1) * LANES)
        later = slice(count + number * LANES, count + (number + 1) * LANES)
        chosen = jnp.where(at_cell == where, 1.0, 0.0).astype(jnp.bfloat16)
        pick[:, columns] = chosen
        pick[:, later] = chosen
        mine = at_line == (line & (INNER - 1))
        for f in range(FIELDS):
            value = jnp.where(mine, incoming[number, f : f + 1, :], 0.0)
            high = value.astype(jnp.bfloat16)
            spread[f * INNER : (f + 1) * INNER, columns] = high
            spread[f * INNER : (f + 1) * INNER, later] = (
                value - high.astype(jnp.float32)
            ).astype(jnp.bfloat16)
        spread[FIELDS * INNER :, columns] = jnp.where(mine, 1.0, 0.0).astype(jnp.bfloat16)
        spread[FIELDS * INNER :, later] = jnp.zeros((INNER, LANES), jnp.bfloat16)
    placed = lax.dot_general(
        spread[...], pick[...], (((1,), (1,)), ((), ())), preferred_element_type=jnp.float32
    )
    for plane in range(4):
        rows = (plane % 2) * width_y
        lanes = slice((plane // 2) * LANES, (plane // 2 + 1) * LANES)
        taken = placed[FIELDS * INNER + rows : FIELDS * INNER + rows + width_y, lanes] > 0.5
        for f in range(FIELDS):
            value = placed[f * INNER + rows : f * INNER + rows + width_y, lanes]
            if plane in (0, 3):
                at_row = 0 if plane == 0 else width_y
                updated[plane, f] = jnp.where(taken, value, rim[f, at_row : at_row + width_y])
                continue
            updated[plane, f] = jnp.where(taken, value, near[plane - 1, f])
            for at_row, y_line in ((63 + plane, 0), (65 + plane, width_y - 1)):
                one = slice(y_line, y_line + 1)
                updated[plane, f, one] = jnp.where(
                    taken[one], value[one], rim[f, at_row : at_row + 1]
                )


def halo(ends, axis, head, tail):
    return (
        lax.ppermute(tail, axis, [(i, i + 1) for i in range(ends)]),
        lax.ppermute(head, axis, [(i + 1, i) for i in range(ends)]),
    )


def shards(
    flow_state,
    source,
    diag_scale,
    flux_jac,
    line_coupling,
    block_inverse,
    active_order,
    active_units,
    donor_cells,
    donor_weights,
    receptor_cells,
):
    f32, i32 = jnp.float32, jnp.int32
    vmem = pl.BlockSpec(memory_space=pltpu.VMEM)
    smem = pl.BlockSpec(memory_space=pltpu.SMEM)
    like = jax.ShapeDtypeStruct
    params = pltpu.CompilerParams(vmem_limit_bytes=32 << 20)
    flow = jnp.transpose(flow_state, (0, 2, 1, 3))
    source = jnp.transpose(source, (0, 2, 1, 3))
    jac = jnp.transpose(flux_jac, (1, 0, 2))
    coupling = jnp.transpose(line_coupling, (1, 0, 2))
    width_x, fields, width_y, length = flow.shape
    cells = donor_cells.reshape(donor_cells.shape[2:])
    weights = donor_weights.reshape(donor_weights.shape[2:])
    receptor = receptor_cells.reshape(receptor_cells.shape[2:])
    blocks = receptor.shape[0]

    x_head, x_tail, y_head, y_tail = pl.pallas_call(
        edges_kernel,
        out_shape=[like((fields, width_y, length), f32)] * 2
        + [like((fields, width_x, length), f32)] * 2,
        in_specs=[vmem],
        out_specs=[vmem] * 4,
        compiler_params=params,
        name="edge_lines",
    )(flow)
    x_prev, x_next = halo(lax.axis_size("blk") - 1, "blk", x_head, x_tail)
    y_prev, y_next = halo(lax.axis_size("bal") - 1, "bal", y_head, y_tail)
    part, near, *rest = pl.pallas_call(
        inner_kernel,
        out_shape=[
            like((blocks, fields, length), f32),
            like((2, fields, width_y, length), f32),
            like((fields, RIM, length), f32),
            like((RIM, length), f32),
            like((RIM, length), f32),
            like((fields, RIM, length), f32),
            like(cells.shape, i32),
            like(cells.shape, f32),
        ],
        in_specs=[smem] * 4 + [vmem] * 6,
        out_specs=[vmem] * 8,
        scratch_shapes=[
            pltpu.VMEM((LANES, LANES), f32),
            pltpu.VMEM(cells.shape, i32),
            pltpu.VMEM((fields * INNER, 2 * LANES), jnp.bfloat16),
        ],
        cost_estimate=pl.CostEstimate(
            flops=10**10, bytes_accessed=3 * 10**6, transcendentals=0
        ),
        compiler_params=params,
        name="inner_lines",
    )(
        jac, coupling, block_inverse, active_units, flow, source, diag_scale,
        active_order.reshape(1, LANES), cells, weights,
    )
    values, rim = pl.pallas_call(
        rim_kernel,
        out_shape=[
            like((blocks, fields, length), f32),
            like((fields, RIM, length), f32),
        ],
        in_specs=[smem] * 3 + [vmem] * 11,
        out_specs=[vmem] * 2,
        scratch_shapes=[
            pltpu.VMEM((fields, RIM, length), f32),
            pltpu.VMEM((fields * RIM, 2 * LANES), jnp.bfloat16),
        ],
        compiler_params=params,
        name="rim_lines",
    )(jac, coupling, block_inverse, x_prev, x_next, y_prev, y_next, part, *rest)
    incoming = lax.all_to_all(values, "blk", split_axis=0, concat_axis=0, tiled=True)
    updated = pl.pallas_call(
        place_kernel,
        out_shape=like(flow.shape, f32),
        in_specs=[vmem] * 4,
        out_specs=vmem,
        scratch_shapes=[
            pltpu.VMEM(((fields + 1) * INNER, 2 * blocks * LANES), jnp.bfloat16),
            pltpu.VMEM((2 * LANES, 2 * blocks * LANES), jnp.bfloat16),
        ],
        compiler_params=params,
        name="place_receptors",
    )(incoming, receptor, near, rim)
    return jnp.transpose(updated, (0, 2, 1, 3))


def solution(mesh):
    placed = (
        P("blk", "bal", None, None),
        P("blk", "bal", None, None),
        P("blk", "bal", None),
        P(),
        P(),
        P(),
        P("blk", "bal", None),
        P("blk", "bal"),
        P("blk", "bal", None, None, None),
        P("blk", "bal", None, None, None),
        P("blk", "bal", None, None),
    )
    return jax.shard_map(
        shards, mesh=mesh, in_specs=placed, out_specs=P("blk", "bal", None, None), check_vma=False
    )
```

time: 741 us -> 60.7 us (0.08)
  local copies, waits for them, and re-layouts: 635 us -> 2.65 us
  starting transfers between devices: 59 us -> 19 us
  waiting for transfers between devices: 30.7 us -> 0.01 us
  Pallas kernels: 0 us -> 21.4 us
  blocking collectives: 0 us -> 16.5 us
  matrix products: 7.83 us -> 0 us
    gather x8 -> x0, local copies, waits for them, and re-layouts: 579 us -> none  [the longest x1 575 us: interpolate(): block_rows[(cell_list // length)[None], field_index, (cell_list % length)...]
    all_to_all x5 -> x0, starting transfers between devices: 45.9 us -> none  [the longest x1 12.9 us: shards(): lax.all_to_all(counts, 'bal', split_axis=0, concat_axis=0, tiled=True)]
    unnamed x23 -> x20, local copies, waits for them, and re-layouts: 46 us -> 2.65 us
    all_to_all x5 -> x0, waiting for transfers between devices: 30 us -> none  [the longest x1 10.2 us: shards(): lax.all_to_all(returning, 'bal', split_axis=0, concat_axis=0, tiled=True)]
    pallas_call x0 -> x4, Pallas kernels: none -> 21.4 us  [the longest x1 9.37 us: shards(): pl.pallas_call(inner_kernel, out_shape=[like((blocks, fields, length), f3...]
    all_to_all x0 -> x1, blocking collectives: none -> 16.5 us  [shards(): lax.all_to_all(values, 'blk', split_axis=0, concat_axis=0, tiled=True)]
    dot_general x16 -> x0, matrix products: 7.83 us -> none  [apply_block(): jnp.einsum('fg,...gp->...fp', matrix, values, precision=lax.Precision.HIG...]
  transfers between devices with their start and end apart: 9 -> 4, of which waited for: 5 -> 0; matrix products, arithmetic and copies ran while one was open for 2% -> 0% of each run, Pallas kernels for 0% -> 16%
where the time goes in v1:
time: 60.7 us; the launch traced here: 60.3 us
  Pallas kernels  21.4 us (35%)
  starting transfers between devices  19 us (31%)
  blocking collectives  16.5 us (27%)
  local copies, waits for them, and re-layouts  2.65 us (4%)
  between operations  0.81 us (1%)
    all_to_all x1, blocking collectives, shards(): lax.all_to_all(values, 'blk', split_axis=0, concat_axis=0, tiled=True)  16.5 us
    ppermute x2, starting transfers between devices, halo(): lax.ppermute(head, axis, [(i + 1, i) for i in range(ends)])  10.8 us
    pallas_call x1, Pallas kernels, shards(): pl.pallas_call(inner_kernel, out_shape=[like((blocks, fields, length), f3...  9.37 us
    pallas_call x1, Pallas kernels, shards(): pl.pallas_call(rim_kernel, out_shape=[like((blocks, fields, length), f32)...  9.3 us
    ppermute x2, starting transfers between devices, halo(): lax.ppermute(tail, axis, [(i, i + 1) for i in range(ends)])  8.18 us
    pallas_call x1, Pallas kernels, shards(): pl.pallas_call(place_kernel, out_shape=like(flow.shape, f32), in_specs=[v...  2.69 us
    unnamed x20, local copies, waits for them, and re-layouts  2.65 us
  transfers between devices with their start and end apart: 4, of which 0 were waited for; matrix products, arithmetic and copies ran while one was open for 0% of the time, Pallas kernels for 16%

profile of v1, /device:TPU:7, one launch (start us, length us, event | category | flops | bytes accessed | tf_op | source)
XLA Modules:
  0.0 60.3 jit_solution(2150819633556788640)
XLA Ops:
  0.0 1.0 %copy-done = f32[4,32,6,128]{3,1,2,0:T(8,128)S(1)} copy-done((f32[4,32,6,128]{3,1,2,0:T(8,128)S(1)}, f32[4,32,6,128]{3,1,2,0:T(8,128)}, u32[]{:S(2)}) %copy-start) | copy-done | bytes 393240
  1.0 0.0 copy-start.1
  1.1 4.1 %collective-permute-start.2 = (f32[6,4,128]{2,1,0:T(4,128)S(1)}, f32[6,4,128]{2,1,0:T(4,128)S(1)}, u32[]{:S(2)}, u32[]{:S(2)}) collective-permute-start(f32[6,4,128]{2,1,0:T(4,128)S(1)} %get-tuple-element.21), channel_id=1, source_target_pairs={{0,1},{1,2},{2,3},{3,4},{4,5},{5,6},{6,7},{7,8},{8,9},{9,10},{10,1... | collective-permute-start | bytes 36872 | tf_op jit(solution)/shard_map/ppermute | solution.py:276
  5.2 8.9 %collective-permute-start.3 = (f32[6,4,128]{2,1,0:T(4,128)S(1)}, f32[6,4,128]{2,1,0:T(4,128)S(1)}, u32[]{:S(2)}, u32[]{:S(2)}) collective-permute-start(f32[6,4,128]{2,1,0:T(4,128)S(1)} %get-tuple-element.22), channel_id=1, source_target_pairs={{1,0},{2,1},{3,2},{4,3},{5,4},{6,5},{7,6},{8,7},{9,8},{10,9},{11,1... | collective-permute-start | bytes 36872 | tf_op jit(solution)/shard_map/ppermute | solution.py:277
  14.1 4.0 %collective-permute-start = (f32[6,32,128]{2,1,0:T(8,128)S(1)}, f32[6,32,128]{2,1,0:T(8,128)S(1)}, u32[]{:S(2)}, u32[]{:S(2)}) collective-permute-start(f32[6,32,128]{2,1,0:T(8,128)S(1)} %get-tuple-element.19), channel_id=1, source_target_pairs={{0,32},{32,64},{64,96},{96,128},{128,160},{160,192},{192,224},{224... | collective-permute-start | bytes 294920 | tf_op jit(solution)/shard_map/ppermute | solution.py:276
  18.1 1.9 %collective-permute-start.1 = (f32[6,32,128]{2,1,0:T(8,128)S(1)}, f32[6,32,128]{2,1,0:T(8,128)S(1)}, u32[]{:S(2)}, u32[]{:S(2)}) collective-permute-start(f32[6,32,128]{2,1,0:T(8,128)S(1)} %get-tuple-element.20), channel_id=1, source_target_pairs={{32,0},{64,32},{96,64},{128,96},{160,128},{192,160},{224,192},{256... | collective-permute-start | bytes 294920 | tf_op jit(solution)/shard_map/ppermute | solution.py:277
  20.7 0.0 copy-start.3
  20.7 0.0 copy-start.9
  20.7 0.0 copy-done.4
  20.7 0.0 copy-done.6
  20.7 0.0 copy-done.7
  20.7 0.0 copy-done.8
  20.8 0.0 copy-done.1
  20.8 0.6 %copy-done.3 = f32[2,6,6]{2,0,1:T(2,128)S(1)} copy-done((f32[2,6,6]{2,0,1:T(2,128)S(1)}, f32[2,6,6]{2,0,1:T(2,128)}, u32[]{:S(2)}) %copy-start.3) | copy-done | bytes 312
  21.4 1.0 %copy-done.5 = f32[4,32,6,128]{3,1,2,0:T(8,128)S(1)} copy-done((f32[4,32,6,128]{3,1,2,0:T(8,128)S(1)}, f32[4,32,6,128]{3,1,2,0:T(8,128)}, u32[]{:S(2)}) %copy-start.5) | copy-done | bytes 393240
  22.4 9.4 %inner_lines.1 = (f32[16,6,128]{2,1,0:T(8,128)S(1)}, f32[2,6,32,128]{3,2,1,0:T(8,128)S(1)}, f32[6,72,128]{2,1,0:T(8,128)S(1)}, f32[72,128]{1,0:T(8,128)S(1)}, f3...) custom-call(f32[6,4,6]{2,1,0:T(4,128)S(1)} %bitcast.11, ...), custom_call_target="tpu_custom_call" | custom-call | flops 10000000000 | bytes 3000000 | tf_op jit(solution)/shard_map/inner_lines/pallas_call | solution.py:320
  31.8 0.0 collective-permute-done.2.y_prev
  31.8 0.0 collective-permute-done.3.y_next
  31.8 0.0 collective-permute-done.x_prev
  31.8 0.0 collective-permute-done.1.x_next
  31.8 9.3 %rim_lines.1 = (f32[16,6,128]{2,1,0:T(8,128)S(1)}, f32[6,72,128]{2,1,0:T(8,128)S(1)}) custom-call(f32[6,4,6]{2,1,0:T(4,128)S(1)} %bitcast.12, f32[6,2,6]{2,1,0:T(2,128)S(1)} %bitcast.15, f32[6,6]{1,0:T(8,128)S(1)} %copy-done.4, f32[6,32,128]{2,1,0:T(8,128)S(1)} %collective-permute-done.x_prev, f32[6,32,128]{2,1,0:T(8,128)S(1)} %collective-permute-done.1.x_next, ...), custom_call_target="tpu_custom_call" | custom-call | tf_op jit(solution)/shard_map/rim_lines/pallas_call | solution.py:348
  41.1 0.0 copy-start.2
  41.1 16.5 %all_to_all.5.incoming = f32[16,6,128]{2,1,0:T(8,128)S(1)} all-to-all(f32[16,6,128]{2,1,0:T(8,128)S(1)} %get-tuple-element.30), channel_id=1, replica_groups=mesh['blk'=16,'bal'=32] {'blk'}, dimensions={0} | all-to-all | bytes 98304 | tf_op jit(solution)/shard_map/all_to_all | solution.py:363
  57.6 2.7 %place_receptors.1 = f32[4,6,32,128]{3,2,1,0:T(8,128)} custom-call(f32[16,6,128]{2,1,0:T(8,128)S(1)} %all_to_all.5.incoming, s32[16,128]{1,0:T(8,128)S(1)} %bitcast.13, f32[2,6,32,128]{3,2,1,0:T(8,128)S(1)} %get-tuple-element.31.near, f32[6,72,128]{2,1,0:T(8,128)S(1)} %get-tuple-element.32.rim), custom_call_target="tpu_custom_call" | custom-call | tf_op jit(solution)/shard_map/place_receptors/pallas_call | solution.py:364
  (9 shorter events, 0.0 us)
Async XLA Ops:
  0.0 1.0 %copy-start = (f32[4,32,6,128]{3,1,2,0:T(8,128)S(1)}, f32[4,32,6,128]{3,1,2,0:T(8,128)}, u32[]{:S(2)}) copy-start(f32[4,32,6,128]{3,1,2,0:T(8,128)} %param.11) | copy-start | bytes 1179652
  1.0 19.7 %copy-start.4 = (f32[6,6]{1,0:T(8,128)S(1)}, f32[6,6]{1,0:T(8,128)}, u32[]{:S(2)}) copy-start(f32[6,6]{1,0:T(8,128)} %inverse.3) | copy-start | bytes 436
  1.0 19.7 %copy-start.6 = (f32[4,32,128]{2,1,0:T(8,128)S(1)}, f32[4,32,128]{2,1,0:T(8,128)}, u32[]{:S(2)}) copy-start(f32[4,32,128]{2,1,0:T(8,128)} %diag.1) | copy-start | bytes 196612
  1.0 19.7 %copy-start.7 = (s32[1,1,8,16,128]{4,3,2,1,0:T(8,128)S(1)}, s32[1,1,8,16,128]{4,3,2,1,0:T(8,128)}, u32[]{:S(2)}) copy-start(s32[1,1,8,16,128]{4,3,2,1,0:T(8,128)} %param.19) | copy-start | bytes 196612
  1.0 19.7 %copy-start.8 = (f32[1,1,8,16,128]{4,3,2,1,0:T(8,128)S(1)}, f32[1,1,8,16,128]{4,3,2,1,0:T(8,128)}, u32[]{:S(2)}) copy-start(f32[1,1,8,16,128]{4,3,2,1,0:T(8,128)} %param.20) | copy-start | bytes 196612
  1.0 19.7 %copy-start.1 = (f32[4,6,6]{2,0,1:T(4,128)S(1)}, f32[4,6,6]{2,0,1:T(4,128)}, u32[]{:S(2)}) copy-start(f32[4,6,6]{2,0,1:T(4,128)} %param.14) | copy-start | bytes 1732
  1.1 30.7 %collective-permute-start.2 = (f32[6,4,128]{2,1,0:T(4,128)S(1)}, f32[6,4,128]{2,1,0:T(4,128)S(1)}, u32[]{:S(2)}, u32[]{:S(2)}) collective-permute-start(f32[6,4,128]{2,1,0:T(4,128)S(1)} %get-tuple-element.21), channel_id=1, source_target_pairs={{0,1},{1,2},{2,3},{3,4},{4,5},{5,6},{6,7},{7,8},{8,9},{9,10},{10,1... | collective-permute-start | bytes 36872 | tf_op jit(solution)/shard_map/ppermute | solution.py:276
  5.2 26.6 %collective-permute-start.3 = (f32[6,4,128]{2,1,0:T(4,128)S(1)}, f32[6,4,128]{2,1,0:T(4,128)S(1)}, u32[]{:S(2)}, u32[]{:S(2)}) collective-permute-start(f32[6,4,128]{2,1,0:T(4,128)S(1)} %get-tuple-element.22), channel_id=1, source_target_pairs={{1,0},{2,1},{3,2},{4,3},{5,4},{6,5},{7,6},{8,7},{9,8},{10,9},{11,1... | collective-permute-start | bytes 36872 | tf_op jit(solution)/shard_map/ppermute | solution.py:277
  14.1 17.7 %collective-permute-start = (f32[6,32,128]{2,1,0:T(8,128)S(1)}, f32[6,32,128]{2,1,0:T(8,128)S(1)}, u32[]{:S(2)}, u32[]{:S(2)}) collective-permute-start(f32[6,32,128]{2,1,0:T(8,128)S(1)} %get-tuple-element.19), channel_id=1, source_target_pairs={{0,32},{32,64},{64,96},{96,128},{128,160},{160,192},{192,224},{224... | collective-permute-start | bytes 294920 | tf_op jit(solution)/shard_map/ppermute | solution.py:276
  18.1 13.7 %collective-permute-start.1 = (f32[6,32,128]{2,1,0:T(8,128)S(1)}, f32[6,32,128]{2,1,0:T(8,128)S(1)}, u32[]{:S(2)}, u32[]{:S(2)}) collective-permute-start(f32[6,32,128]{2,1,0:T(8,128)S(1)} %get-tuple-element.20), channel_id=1, source_target_pairs={{32,0},{64,32},{96,64},{128,96},{160,128},{192,160},{224,192},{256... | collective-permute-start | bytes 294920 | tf_op jit(solution)/shard_map/ppermute | solution.py:277
  20.7 0.7 %copy-start.3 = (f32[2,6,6]{2,0,1:T(2,128)S(1)}, f32[2,6,6]{2,0,1:T(2,128)}, u32[]{:S(2)}) copy-start(f32[2,6,6]{2,0,1:T(2,128)} %param.15) | copy-start | bytes 868
  20.7 0.7 %copy-start.9 = (s32[1,1,128]{2,1,0:T(1,128)S(1)}, s32[1,1,128]{2,1,0:T(1,128)}, u32[]{:S(2)}) copy-start(s32[1,1,128]{2,1,0:T(1,128)} %param.17) | copy-start | bytes 1540
  21.4 1.0 %copy-start.5 = (f32[4,32,6,128]{3,1,2,0:T(8,128)S(1)}, f32[4,32,6,128]{3,1,2,0:T(8,128)}, u32[]{:S(2)}) copy-start(f32[4,32,6,128]{3,1,2,0:T(8,128)} %param.12) | copy-start | bytes 1179652
  41.1 16.5 %copy-start.2 = (s32[1,1,16,128]{3,2,1,0:T(8,128)S(1)}, s32[1,1,16,128]{3,2,1,0:T(8,128)}, u32[]{:S(2)}) copy-start(s32[1,1,16,128]{3,2,1,0:T(8,128)} %param.21) | copy-start | bytes 24580

commit v2 on v1

v2 whole, which is shorter than its diff:
```python
import functools

import jax
import jax.numpy as jnp
from jax import lax
from jax.experimental import pallas as pl
from jax.experimental.pallas import tpu as pltpu
from jax.sharding import PartitionSpec as P

SWEEPS = 4
FIELDS = 6
DONORS = 8
LANES = 128
INNER = 64
RIM = 72
NOWHERE = 255
BY_MATRIX = 4
STEPS = 1048000.0


def apply(matrix, values):
    out = []
    for f in range(FIELDS):
        total = matrix(f, 0) * values[0]
        for g in range(1, FIELDS):
            total = total + matrix(f, g) * values[g]
        out.append(total)
    return out


def solve(residual, scale_inv, matrices):
    lane = lax.broadcasted_iota(jnp.int32, residual[0].shape, 1)
    first, last = lane == 0, lane == LANES - 1
    base = apply(lambda f, g: matrices[3, f, g], residual)
    base = [value * scale_inv for value in base]
    correction = base
    for _ in range(SWEEPS - 1):
        total = [None] * FIELDS
        for g in range(FIELDS):
            down = jnp.where(first, 0.0, pltpu.roll(correction[g], 1, 1))
            up = jnp.where(last, 0.0, pltpu.roll(correction[g], LANES - 1, 1))
            for f in range(FIELDS):
                term = matrices[1, f, g] * down + matrices[2, f, g] * up
                total[f] = term if g == 0 else total[f] + term
        correction = [base[f] - scale_inv * total[f] for f in range(FIELDS)]
    return correction


def fill_table(table, rows, field, first, values):
    high = values.astype(jnp.bfloat16)
    low = (values - high.astype(jnp.float32)).astype(jnp.bfloat16)
    count = values.shape[0]
    table[field * rows + first : field * rows + first + count, 0:LANES] = high
    table[field * rows + first : field * rows + first + count, LANES : 2 * LANES] = low


def fill_words(words, scales, corrected):
    whole = []
    for f in range(FIELDS):
        largest = jnp.max(jnp.max(jnp.abs(corrected(f)), axis=0, keepdims=True), axis=1, keepdims=True)
        scale = jnp.broadcast_to(jnp.maximum(largest, 1e-30), (8, LANES))
        scales[f] = scale * (1.0 / (STEPS * 2048.0))
        factor = (STEPS / scale)[0:1]
        whole.append(jnp.round(corrected(f) * factor).astype(jnp.int32))
    parts = []
    for f in (4, 5):
        upper = (whole[f] + 512) >> 10
        parts += [upper, whole[f] - (upper << 10)]
    for word in range(4):
        words[word] = (whole[word] << 11) + parts[word]


def gather_by_lane(words, rows, cell, share, total):
    below = lax.broadcasted_iota(jnp.int32, (8, LANES), 0)
    cell = jnp.broadcast_to(cell, (8, LANES))
    pos = cell & (LANES - 1)
    line = (cell >> 7) - below
    here = ((line & 7) == 0) & (line < rows) & (line >= 0)
    share = jnp.where(here, jnp.broadcast_to(share, (8, LANES)), 0.0)
    hit = [None] * 4
    for first in range(0, rows, 8):
        chosen = line == first
        for word in range(4):
            found = jnp.take_along_axis(
                words[word, first : first + 8], pos, axis=1, mode="promise_in_bounds"
            )
            hit[word] = found if first == 0 else jnp.where(chosen, found, hit[word])
    low = [(value << 21).astype(jnp.float32) for value in hit]
    found = [value.astype(jnp.float32) for value in hit]
    found += [low[0] + low[1] * (1.0 / 1024), low[2] + low[3] * (1.0 / 1024)]
    return [
        value * share if total is None else total[f] + value * share
        for f, value in enumerate(found)
    ]


def small(numbers):
    return numbers.astype(jnp.float32).astype(jnp.bfloat16)


def gather(table, words, scales, rows, cells, shares, number):
    at_cell = small(lax.broadcasted_iota(jnp.int32, (LANES, 2 * LANES), 0))
    at_line = lax.broadcasted_iota(jnp.int32, (rows, 2 * LANES), 0)
    one, zero = jnp.bfloat16(1), jnp.bfloat16(0)
    total = [None] * FIELDS
    for k in range(0, BY_MATRIX, 2):
        cell = jnp.concatenate([cells[k + i, pl.ds(number, 1), :] for i in (0, 1)], axis=1)
        share = jnp.concatenate([shares[k + i, pl.ds(number, 1), :] for i in (0, 1)], axis=1)
        pick = jnp.where(at_cell == small(cell & (LANES - 1)), one, zero)
        found = jnp.dot(
            table[...], jnp.concatenate([pick, pick], axis=0), preferred_element_type=jnp.float32
        )
        weight = jnp.where(at_line == (cell >> 7), share, 0.0)
        for f in range(FIELDS):
            part = found[f * rows : (f + 1) * rows] * weight
            part = jnp.sum(part.reshape(rows // 8, 8, 2 * LANES), axis=0)
            total[f] = part if k == 0 else total[f] + part
    by_lane = None
    for k in range(BY_MATRIX, DONORS):
        by_lane = gather_by_lane(
            words, rows, cells[k, pl.ds(number, 1), :], shares[k, pl.ds(number, 1), :], by_lane
        )
    return [
        jnp.sum(
            value[:, :LANES] + value[:, LANES:] + by_lane[f] * scales[f], axis=0, keepdims=True
        )
        for f, value in enumerate(total)
    ]


def load_kernel(
    jac_in, coupling_in, inverse_in, flow_in, source_in, diag_in, cells_in, weights_in,
    x_head, x_tail, y_head, y_tail, flow, source, diag, cells, weights, matrices,
    jac, coupling, inverse, done,
):
    width_x, _, width_y, _ = flow.shape
    copies = [
        pltpu.make_async_copy(origin, target, done.at[number])
        for number, (origin, target) in enumerate(
            (
                (flow_in, flow),
                (jac_in, jac),
                (coupling_in, coupling),
                (inverse_in, inverse),
                (flow_in.at[0], x_head),
                (flow_in.at[width_x - 1], x_tail),
                (source_in, source),
                (diag_in, diag),
                (cells_in, cells),
                (weights_in, weights),
            )
        )
    ]
    for copy in copies:
        copy.start()
    for copy in copies[1:4]:
        copy.wait()
    for f in range(FIELDS):
        for g in range(FIELDS):
            for side in range(4):
                matrices[4 + side, f, g] = jac[f, side, g]
            matrices[0, f, g] = jac[f, 0, g] + jac[f, 1, g] + jac[f, 2, g] + jac[f, 3, g]
            matrices[3, f, g] = inverse[f, g]
            for side in (0, 1):
                total = inverse[f, 0] * coupling[0, side, g]
                for h in range(1, FIELDS):
                    total = total + inverse[f, h] * coupling[h, side, g]
                matrices[1 + side, f, g] = total
    copies[0].wait()
    for f in range(FIELDS):
        for x in range(width_x):
            y_head[f, x : x + 1] = flow[x, f, 0:1]
            y_tail[f, x : x + 1] = flow[x, f, width_y - 1 : width_y]
    for copy in copies[4:]:
        copy.wait()


def inner_kernel(
    matrices, units, flow, source, diag, order, cells, weights,
    values, near, rim_residual, rim_scale, rim_live, rim_flow, rim_cells, shares,
    live, inner_cells, table, words, scales,
):
    width_y = flow.shape[2]
    blocks = cells.shape[1]
    line = lax.broadcasted_iota(jnp.int32, (LANES, LANES), 0)
    place = lax.broadcasted_iota(jnp.int32, (LANES, LANES), 1)
    hit = (line == order[...]) & (place < units[0, 0] * 32)
    live[...] = jnp.broadcast_to(
        jnp.max(jnp.where(hit, 1.0, 0.0), axis=1, keepdims=True), (LANES, LANES)
    )
    row = lax.broadcasted_iota(jnp.int32, (width_y, LANES), 0)

    cell = cells[...]
    at = cell >> 7
    x, y = at >> 5, at & 31
    middle = (x == 1) | (x == 2)
    edge = middle & ((y == 0) | (y == width_y - 1))
    pos = cell & (LANES - 1)
    inner_cells[...] = (jnp.where(middle & ~edge, at - 32, NOWHERE) << 7) + pos
    on_edge = 64 + (x - 1) + jnp.where(y == 0, 0, 2)
    on_rim = jnp.where(x == 0, at, jnp.where(x == 3, at - 64, NOWHERE))
    rim_cells[...] = (jnp.where(edge, on_edge, on_rim) << 7) + pos
    weight = weights[...]
    shares[...] = weight / jnp.sum(weight, axis=0, keepdims=True)

    def residual_of(plane):
        total = [source[plane, f] for f in range(FIELDS)]
        for g in range(FIELDS):
            here = flow[plane, g]
            left = flow[plane - 1, g] if plane > 0 else None
            right = flow[plane + 1, g] if plane < 3 else None
            before = jnp.where(row == 0, 0.0, pltpu.roll(here, 1, 0))
            after = jnp.where(row == width_y - 1, 0.0, pltpu.roll(here, width_y - 1, 0))
            for f in range(FIELDS):
                value = total[f] - matrices[0, f, g] * here
                if left is not None:
                    value = value + matrices[4, f, g] * left
                if right is not None:
                    value = value + matrices[5, f, g] * right
                total[f] = value + matrices[6, f, g] * before + matrices[7, f, g] * after
        return total

    for number, plane in enumerate((0, 3)):
        residual = residual_of(plane)
        rows = slice(number * width_y, (number + 1) * width_y)
        for f in range(FIELDS):
            rim_residual[f, rows] = residual[f]
            rim_flow[f, rows] = flow[plane, f]
        rim_scale[rows] = 1.0 / diag[plane]
        rim_live[rows] = live[plane * width_y : (plane + 1) * width_y]
    rim_scale[RIM - 8 : RIM] = jnp.ones((8, LANES), jnp.float32)
    rim_live[RIM - 8 : RIM] = jnp.zeros((8, LANES), jnp.float32)
    for f in range(FIELDS):
        rim_residual[f, RIM - 8 : RIM] = jnp.zeros((8, LANES), jnp.float32)
        rim_flow[f, RIM - 8 : RIM] = jnp.zeros((8, LANES), jnp.float32)
    for number, plane in enumerate((1, 2)):
        residual = residual_of(plane)
        scale = 1.0 / diag[plane]
        alive = live[plane * width_y : (plane + 1) * width_y]
        for at_row, y_line in ((64 + number, 0), (66 + number, width_y - 1)):
            for f in range(FIELDS):
                rim_residual[f, at_row : at_row + 1] = residual[f][y_line : y_line + 1]
                rim_flow[f, at_row : at_row + 1] = flow[plane, f, y_line : y_line + 1]
            rim_scale[at_row : at_row + 1] = scale[y_line : y_line + 1]
            rim_live[at_row : at_row + 1] = alive[y_line : y_line + 1]
        correction = solve(residual, scale, matrices)
        for f in range(FIELDS):
            corrected = flow[plane, f] + jnp.where(alive > 0.5, correction[f], 0.0)
            near[number, f] = corrected
            fill_table(table, INNER, f, number * width_y, corrected)

    fill_words(
        words, scales, lambda f: jnp.concatenate([near[0, f], near[1, f]], axis=0)
    )

    @pl.loop(0, blocks, unroll=4)
    def _(number):
        found = gather(table, words, scales, INNER, inner_cells, shares, number)
        for f in range(FIELDS):
            values[number, f : f + 1, :] = found[f]


def rim_kernel(
    matrices, x_prev, x_next, y_prev, y_next,
    part, rim_residual, rim_scale, rim_live, rim_flow, rim_cells, shares,
    values, rim, residual, table, words, scales,
):
    width_y = x_prev.shape[1]
    blocks = rim_cells.shape[1]
    for number, (side, halo) in enumerate(((0, x_prev), (1, x_next))):
        rows = slice(number * width_y, (number + 1) * width_y)
        added = apply(lambda f, g: matrices[4 + side, f, g], [halo[g] for g in range(FIELDS)])
        for f in range(FIELDS):
            residual[f, rows] = rim_residual[f, rows] + added[f]
    for number, (side, halo) in enumerate(((2, y_prev), (3, y_next))):
        added = apply(lambda f, g: matrices[4 + side, f, g], [halo[g] for g in range(FIELDS)])
        for f in range(FIELDS):
            at_row = 64 + 2 * number
            residual[f, at_row : at_row + 2] = (
                rim_residual[f, at_row : at_row + 2] + added[f][1:3]
            )
            for at_row, x in ((number * (width_y - 1), 0), (width_y + number * (width_y - 1), 3)):
                residual[f, at_row : at_row + 1] = (
                    residual[f, at_row : at_row + 1] + added[f][x : x + 1]
                )
    for f in range(FIELDS):
        residual[f, RIM - 4 : RIM] = jnp.zeros((4, LANES), jnp.float32)
    for first in range(0, RIM, 24):
        rows = slice(first, first + 24)
        correction = solve(
            [residual[f, rows] for f in range(FIELDS)], rim_scale[rows], matrices
        )
        alive = rim_live[rows] > 0.5
        for f in range(FIELDS):
            corrected = rim_flow[f, rows] + jnp.where(alive, correction[f], 0.0)
            rim[f, rows] = corrected
            fill_table(table, RIM, f, first, corrected)

    fill_words(words, scales, lambda f: rim[f])

    @pl.loop(0, blocks, unroll=4)
    def _(number):
        found = gather(table, words, scales, RIM, rim_cells, shares, number)
        for f in range(FIELDS):
            values[number, f : f + 1, :] = found[f] + part[number, f : f + 1, :]


def prepare_kernel(receptor, near, rim, base, lines, pick):
    blocks = receptor.shape[0]
    width_y = near.shape[2]
    at_line = lax.broadcasted_iota(jnp.int32, (INNER, LANES), 0)
    at_cell = lax.broadcasted_iota(jnp.int32, (LANES, LANES), 1)
    for number in range(blocks):
        cell = receptor[number : number + 1, :]
        line = cell >> 7
        where = ((line >> 6) << 7) + (cell & (LANES - 1))
        span = slice(number * LANES, (number + 1) * LANES)
        lines[:, span] = jnp.where(at_line == (line & (INNER - 1)), 1.0, 0.0).astype(jnp.bfloat16)
        where = jnp.transpose(jnp.broadcast_to(where, (LANES, LANES)))
        for half in (0, 1):
            pick[span, half * LANES : (half + 1) * LANES] = jnp.where(
                at_cell + half * LANES == where, 1.0, 0.0
            ).astype(jnp.bfloat16)
    taken = jnp.dot(lines[...], pick[...], preferred_element_type=jnp.float32)
    for plane in range(4):
        rows = (plane % 2) * width_y
        lanes = slice((plane // 2) * LANES, (plane // 2 + 1) * LANES)
        free = taken[rows : rows + width_y, lanes] < 0.5
        for f in range(FIELDS):
            if plane in (0, 3):
                at_row = 0 if plane == 0 else width_y
                base[plane, f] = jnp.where(free, rim[f, at_row : at_row + width_y], 0.0)
                continue
            base[plane, f] = jnp.where(free, near[plane - 1, f], 0.0)
            for at_row, y_line in ((63 + plane, 0), (65 + plane, width_y - 1)):
                one = slice(y_line, y_line + 1)
                base[plane, f, one] = jnp.where(free[one], rim[f, at_row : at_row + 1], 0.0)


def place_kernel(incoming, base, lines, pick, updated, high, low):
    blocks = incoming.shape[0]
    width_y = base.shape[2]
    for number in range(blocks):
        span = slice(number * LANES, (number + 1) * LANES)
        value = incoming[number]
        upper = value.astype(jnp.bfloat16).astype(jnp.float32)
        lower = value - upper
        for f in range(FIELDS):
            for part, target in ((upper, high), (lower, low)):
                wide = jnp.broadcast_to(part[f : f + 1], (16, LANES)).astype(jnp.bfloat16)
                for first in range(0, INNER, 16):
                    target[f * INNER + first : f * INNER + first + 16, span] = (
                        lines[first : first + 16, span] * wide
                    )
    placed = jnp.dot(high[...], pick[...], preferred_element_type=jnp.float32)
    placed = placed + jnp.dot(low[...], pick[...], preferred_element_type=jnp.float32)
    for plane in range(4):
        rows = (plane % 2) * width_y
        lanes = slice((plane // 2) * LANES, (plane // 2 + 1) * LANES)
        for f in range(FIELDS):
            updated[plane, f] = (
                base[plane, f] + placed[f * INNER + rows : f * INNER + rows + width_y, lanes]
            )


def halo(ends, axis, head, tail):
    return (
        lax.ppermute(tail, axis, [(i, i + 1) for i in range(ends)]),
        lax.ppermute(head, axis, [(i + 1, i) for i in range(ends)]),
    )


def shards(
    flow_state,
    source,
    diag_scale,
    flux_jac,
    line_coupling,
    block_inverse,
    active_order,
    active_units,
    donor_cells,
    donor_weights,
    receptor_cells,
):
    f32, i32 = jnp.float32, jnp.int32
    vmem = pl.BlockSpec(memory_space=pltpu.VMEM)
    smem = pl.BlockSpec(memory_space=pltpu.SMEM)
    like = jax.ShapeDtypeStruct
    params = pltpu.CompilerParams(vmem_limit_bytes=32 << 20)
    flow = jnp.transpose(flow_state, (0, 2, 1, 3))
    source = jnp.transpose(source, (0, 2, 1, 3))
    jac = jnp.transpose(flux_jac, (1, 0, 2))
    coupling = jnp.transpose(line_coupling, (1, 0, 2))
    width_x, fields, width_y, length = flow.shape
    cells = donor_cells.reshape(donor_cells.shape[2:])
    weights = donor_weights.reshape(donor_weights.shape[2:])
    receptor = receptor_cells.reshape(receptor_cells.shape[2:])
    blocks = receptor.shape[0]

    outside = pl.BlockSpec(memory_space=pltpu.HBM)
    raw = [
        pltpu.with_memory_space_constraint(array, pltpu.HBM)
        for array in (jac, coupling, block_inverse, flow, source, diag_scale, cells, weights)
    ]
    x_head, x_tail, y_head, y_tail, flow, source, diag, cells, weights, matrices = pl.pallas_call(
        load_kernel,
        out_shape=[like((fields, width_y, length), f32)] * 2
        + [like((fields, width_x, length), f32)] * 2
        + [like(array.shape, array.dtype) for array in raw[3:]]
        + [like((8, fields, fields), f32)],
        in_specs=[outside] * 8,
        out_specs=[vmem] * 9 + [smem],
        scratch_shapes=[
            pltpu.SMEM(jac.shape, f32),
            pltpu.SMEM(coupling.shape, f32),
            pltpu.SMEM(block_inverse.shape, f32),
            pltpu.SemaphoreType.DMA((10,)),
        ],
        compiler_params=params,
        name="load_block",
    )(*raw)
    x_prev, x_next = halo(lax.axis_size("blk") - 1, "blk", x_head, x_tail)
    y_prev, y_next = halo(lax.axis_size("bal") - 1, "bal", y_head, y_tail)
    part, near, *rest = pl.pallas_call(
        inner_kernel,
        out_shape=[
            like((blocks, fields, length), f32),
            like((2, fields, width_y, length), f32),
            like((fields, RIM, length), f32),
            like((RIM, length), f32),
            like((RIM, length), f32),
            like((fields, RIM, length), f32),
            like(cells.shape, i32),
            like(cells.shape, f32),
        ],
        in_specs=[smem] * 2 + [vmem] * 6,
        out_specs=[vmem] * 8,
        scratch_shapes=[
            pltpu.VMEM((LANES, LANES), f32),
            pltpu.VMEM(cells.shape, i32),
            pltpu.VMEM((fields * INNER, 2 * LANES), jnp.bfloat16),
            pltpu.VMEM((4, INNER, LANES), i32),
            pltpu.VMEM((fields, 8, LANES), f32),
        ],
        cost_estimate=pl.CostEstimate(
            flops=10**10, bytes_accessed=3 * 10**6, transcendentals=0
        ),
        compiler_params=params,
        name="inner_lines",
    )(
        matrices, active_units, flow, source, diag,
        active_order.reshape(1, LANES), cells, weights,
    )
    values, rim = pl.pallas_call(
        rim_kernel,
        out_shape=[
            like((blocks, fields, length), f32),
            like((fields, RIM, length), f32),
        ],
        in_specs=[smem] + [vmem] * 11,
        out_specs=[vmem] * 2,
        scratch_shapes=[
            pltpu.VMEM((fields, RIM, length), f32),
            pltpu.VMEM((fields * RIM, 2 * LANES), jnp.bfloat16),
            pltpu.VMEM((4, RIM, LANES), i32),
            pltpu.VMEM((fields, 8, LANES), f32),
        ],
        compiler_params=params,
        name="rim_lines",
    )(matrices, x_prev, x_next, y_prev, y_next, part, *rest)
    incoming = lax.all_to_all(values, "blk", split_axis=0, concat_axis=0, tiled=True)
    base, lines, pick = pl.pallas_call(
        prepare_kernel,
        out_shape=[
            like(flow.shape, f32),
            like((INNER, blocks * LANES), jnp.bfloat16),
            like((blocks * LANES, 2 * LANES), jnp.bfloat16),
        ],
        in_specs=[vmem] * 3,
        out_specs=[vmem] * 3,
        cost_estimate=pl.CostEstimate(
            flops=5 * 10**9, bytes_accessed=3 * 10**6, transcendentals=0
        ),
        compiler_params=params,
        name="prepare_receptors",
    )(receptor, near, rim)
    updated = pl.pallas_call(
        place_kernel,
        out_shape=like(flow.shape, f32),
        in_specs=[vmem] * 4,
        out_specs=vmem,
        scratch_shapes=[pltpu.VMEM((fields * INNER, blocks * LANES), jnp.bfloat16)] * 2,
        compiler_params=params,
        name="place_receptors",
    )(incoming, base, lines, pick)
    return jnp.transpose(updated, (0, 2, 1, 3))


def solution(mesh):
    placed = (
        P("blk", "bal", None, None),
        P("blk", "bal", None, None),
        P("blk", "bal", None),
        P(),
        P(),
        P(),
        P("blk", "bal", None),
        P("blk", "bal"),
        P("blk", "bal", None, None, None),
        P("blk", "bal", None, None, None),
        P("blk", "bal", None, None),
    )
    return jax.shard_map(
        shards, mesh=mesh, in_specs=placed, out_specs=P("blk", "bal", None, None), check_vma=False
    )
```

time: 60.7 us -> 54.3 us (0.89)
  blocking collectives: 16.5 us -> 0 us
  starting transfers between devices: 19 us -> 27.8 us
  waiting for transfers between devices: 0.01 us -> 7.17 us
  Pallas kernels: 21.4 us -> 17.6 us
  local copies, waits for them, and re-layouts: 2.65 us -> 0.65 us
    all_to_all x1 -> x0, blocking collectives: 16.5 us -> none  [shards(): lax.all_to_all(values, 'blk', split_axis=0, concat_axis=0, tiled=True)]
    all_to_all x0 -> x1, starting transfers between devices: none -> 9.03 us  [shards(): lax.all_to_all(values, 'blk', split_axis=0, concat_axis=0, tiled=True)]
    all_to_all x0 -> x1, waiting for transfers between devices: none -> 7.16 us  [shards(): lax.all_to_all(values, 'blk', split_axis=0, concat_axis=0, tiled=True)]
    pallas_call x1 -> x2, Pallas kernels: 0.03 us -> 3.57 us  [the longest x1 2.94 us: shards(): pl.pallas_call(load_kernel, out_shape=[like((fields, width_y, length), f3...]
    pallas_call x1, Pallas kernels: 9.37 us -> 6.01 us  [shards(): pl.pallas_call(inner_kernel, out_shape=[like((blocks, fields, length), f3...]
    pallas_call x1, Pallas kernels: 9.3 us -> 6.18 us  [shards(): pl.pallas_call(rim_kernel, out_shape=[like((blocks, fields, length), f32)...]
    unnamed x20 -> x4, local copies, waits for them, and re-layouts: 2.65 us -> 0.65 us
    pallas_call x1, Pallas kernels: 2.69 us -> 1.8 us  [shards(): pl.pallas_call(place_kernel, out_shape=like(flow.shape, f32), in_specs=[v...]
  transfers between devices with their start and end apart: 4 -> 5, of which waited for: 0 -> 1; matrix products, arithmetic and copies ran while one was open for 0% -> 0% of each run, Pallas kernels for 16% -> 12%
where the time goes in v2:
time: 54.3 us; the launch traced here: 54 us
  starting transfers between devices  27.8 us (51%)
  Pallas kernels  17.6 us (32%)
  waiting for transfers between devices  7.17 us (13%)
  between operations  0.74 us (1%)
  local copies, waits for them, and re-layouts  0.65 us (1%)
    ppermute x2, starting transfers between devices, halo(): lax.ppermute(head, axis, [(i + 1, i) for i in range(ends)])  10.8 us
    all_to_all x1, starting transfers between devices, shards(): lax.all_to_all(values, 'blk', split_axis=0, concat_axis=0, tiled=True)  9.03 us
    ppermute x2, starting transfers between devices, halo(): lax.ppermute(tail, axis, [(i, i + 1) for i in range(ends)])  8.05 us
    all_to_all x1, waiting for transfers between devices, shards(): lax.all_to_all(values, 'blk', split_axis=0, concat_axis=0, tiled=True)  7.16 us
    pallas_call x1, Pallas kernels, shards(): pl.pallas_call(rim_kernel, out_shape=[like((blocks, fields, length), f32)...  6.18 us
    pallas_call x1, Pallas kernels, shards(): pl.pallas_call(inner_kernel, out_shape=[like((blocks, fields, length), f3...  6.01 us
    pallas_call x1, Pallas kernels, shards(): pl.pallas_call(load_kernel, out_shape=[like((fields, width_y, length), f3...  2.94 us
    pallas_call x1, Pallas kernels, shards(): pl.pallas_call(place_kernel, out_shape=like(flow.shape, f32), in_specs=[v...  1.8 us
  transfers between devices with their start and end apart: 5, of which 1 were waited for; matrix products, arithmetic and copies ran while one was open for 0% of the time, Pallas kernels for 12%

profile of v2, /device:TPU:7, one launch (start us, length us, event | category | flops | bytes accessed | tf_op | source)
XLA Modules:
  0.0 54.0 jit_solution(4729628111792940211)
XLA Ops:
  0.0 2.9 %load_block.1 = (f32[6,32,128]{2,1,0:T(8,128)S(1)}, f32[6,32,128]{2,1,0:T(8,128)S(1)}, f32[6,4,128]{2,1,0:T(4,128)S(1)}, f32[6,4,128]{2,1,0:T(4,128)S(1)}, f32[4...) custom-call(f32[6,4,6]{2,1,0:T(4,128)} %bitcast.15, ...), custom_call_target="tpu_custom_call" | custom-call | tf_op jit(solution)/shard_map/load_block/pallas_call | solution.py:406
  2.9 4.0 %collective-permute-start.2 = (f32[6,4,128]{2,1,0:T(4,128)S(1)}, f32[6,4,128]{2,1,0:T(4,128)S(1)}, u32[]{:S(2)}, u32[]{:S(2)}) collective-permute-start(f32[6,4,128]{2,1,0:T(4,128)S(1)} %get-tuple-element.31), channel_id=1, source_target_pairs={{0,1},{1,2},{2,3},{3,4},{4,5},{5,6},{6,7},{7,8},{8,9},{9,10},{10,1... | collective-permute-start | bytes 36872 | tf_op jit(solution)/shard_map/ppermute | solution.py:368
  7.0 8.9 %collective-permute-start.3 = (f32[6,4,128]{2,1,0:T(4,128)S(1)}, f32[6,4,128]{2,1,0:T(4,128)S(1)}, u32[]{:S(2)}, u32[]{:S(2)}) collective-permute-start(f32[6,4,128]{2,1,0:T(4,128)S(1)} %get-tuple-element.32), channel_id=1, source_target_pairs={{1,0},{2,1},{3,2},{4,3},{5,4},{6,5},{7,6},{8,7},{9,8},{10,9},{11,1... | collective-permute-start | bytes 36872 | tf_op jit(solution)/shard_map/ppermute | solution.py:369
  15.8 4.0 %collective-permute-start = (f32[6,32,128]{2,1,0:T(8,128)S(1)}, f32[6,32,128]{2,1,0:T(8,128)S(1)}, u32[]{:S(2)}, u32[]{:S(2)}) collective-permute-start(f32[6,32,128]{2,1,0:T(8,128)S(1)} %get-tuple-element.29), channel_id=1, source_target_pairs={{0,32},{32,64},{64,96},{96,128},{128,160},{160,192},{192,224},{224... | collective-permute-start | bytes 294920 | tf_op jit(solution)/shard_map/ppermute | solution.py:368
  19.9 1.9 %collective-permute-start.1 = (f32[6,32,128]{2,1,0:T(8,128)S(1)}, f32[6,32,128]{2,1,0:T(8,128)S(1)}, u32[]{:S(2)}, u32[]{:S(2)}) collective-permute-start(f32[6,32,128]{2,1,0:T(8,128)S(1)} %get-tuple-element.30), channel_id=1, source_target_pairs={{32,0},{64,32},{96,64},{128,96},{160,128},{192,160},{224,192},{256... | collective-permute-start | bytes 294920 | tf_op jit(solution)/shard_map/ppermute | solution.py:369
  22.4 0.0 copy-start.1
  22.5 0.6 %copy-done.1 = s32[1,1,128]{2,1,0:T(1,128)S(1)} copy-done((s32[1,1,128]{2,1,0:T(1,128)S(1)}, s32[1,1,128]{2,1,0:T(1,128)}, u32[]{:S(2)}) %copy-start.1) | copy-done | bytes 536
  23.1 6.0 %inner_lines.1 = (f32[16,6,128]{2,1,0:T(8,128)S(1)}, f32[2,6,32,128]{3,2,1,0:T(8,128)S(1)}, f32[6,72,128]{2,1,0:T(8,128)S(1)}, f32[72,128]{1,0:T(8,128)S(1)}, f3...) custom-call(f32[8,6,6]{2,1,0:T(8,128)S(1)} %get-tuple-element.28.matrice, ...), custom_call_target="tpu_custom_call" | custom-call | flops 10000000000 | bytes 3000000 | tf_op jit(solution)/shard_map/inner_lines/pallas_call | solution.py:425
  29.1 0.0 collective-permute-done.2.y_prev
  29.1 0.0 collective-permute-done.3.y_next
  29.1 0.0 collective-permute-done.x_prev
  29.1 0.0 collective-permute-done.1.x_next
  29.2 6.2 %rim_lines.1 = (f32[16,6,128]{2,1,0:T(8,128)}, f32[6,72,128]{2,1,0:T(8,128)S(1)}) custom-call(f32[8,6,6]{2,1,0:T(8,128)S(1)} %get-tuple-element.28.matrices, f32[6,32,128]{2,1,0:T(8,128)S(1)} %collective-permute-done.x_prev, f32[6,32,128]{2,1,0:T(8,128)S(1)} %collective-permute-done.1.x_next, f32[6,4,128]{2,1,0:T(4,128)S(1)} %collective-permute-done.2.y_prev, ...), custom_call_target="tpu_custom_call" | custom-call | tf_op jit(solution)/shard_map/rim_lines/pallas_call | solution.py:455
  35.3 0.0 copy-start
  35.3 9.0 %all-to-all-start = ((f32[16,6,128]{2,1,0:T(8,128)}), f32[16,6,128]{2,1,0:T(8,128)S(1)}, u32[]{:S(2)}, u32[]{:S(2)}) async-start(f32[16,6,128]{2,1,0:T(8,128)} %get-tuple-element.45), calls=%async_computation | async-start | bytes 131072 | tf_op jit(solution)/shard_map/all_to_all | solution.py:472
  44.4 0.0 copy-done
  44.4 0.6 %prepare_receptors.1 = (f32[4,6,32,128]{3,2,1,0:T(8,128)S(1)}, bf16[64,2048]{1,0:T(8,128)(2,1)S(1)}, bf16[2048,256]{1,0:T(8,128)(2,1)S(1)}) custom-call(s32[16,128]{1,0:T(8,128)S(1)} %bitcast.9, f32[2,6,32,128]{3,2,1,0:T(8,128)S(1)} %get-tuple-element.46.near, f32[6,72,128]{2,1,0:T(8,128)S(1)} %get-tuple-element.47.rim), custom_call_target="tpu_custom_call" | custom-call | flops 5000000000 | bytes 3000000 | tf_op jit(solution)/shard_map/prepare_receptors/pallas_call | solution.py:473
  45.0 7.2 %all-to-all-done.incoming = f32[16,6,128]{2,1,0:T(8,128)S(1)} async-done(((f32[16,6,128]{2,1,0:T(8,128)}), f32[16,6,128]{2,1,0:T(8,128)S(1)}, u32[]{:S(2)}, u32[]{:S(2)}) %all-to-all-start) | async-done | bytes 49184 | tf_op jit(solution)/shard_map/all_to_all | solution.py:472
  52.2 1.8 %place_receptors.1 = f32[4,6,32,128]{3,2,1,0:T(8,128)} custom-call(f32[16,6,128]{2,1,0:T(8,128)S(1)} %all-to-all-done.incoming, f32[4,6,32,128]{3,2,1,0:T(8,128)S(1)} %get-tuple-element.48.base, bf16[64,2048]{1,0:T(8,128)(2,1)S(1)} %get-tuple-element.49.lines, bf16[2048,256]{1,0:T(8,128)(2,1)S(1)} %get-tuple-element.50.pick), custom_call_target="tpu_custom_call" | custom-call | tf_op jit(solution)/shard_map/place_receptors/pallas_call | solution.py:488
Async XLA Ops:
  2.9 26.2 %collective-permute-start.2 = (f32[6,4,128]{2,1,0:T(4,128)S(1)}, f32[6,4,128]{2,1,0:T(4,128)S(1)}, u32[]{:S(2)}, u32[]{:S(2)}) collective-permute-start(f32[6,4,128]{2,1,0:T(4,128)S(1)} %get-tuple-element.31), channel_id=1, source_target_pairs={{0,1},{1,2},{2,3},{3,4},{4,5},{5,6},{6,7},{7,8},{8,9},{9,10},{10,1... | collective-permute-start | bytes 36872 | tf_op jit(solution)/shard_map/ppermute | solution.py:368
  7.0 22.2 %collective-permute-start.3 = (f32[6,4,128]{2,1,0:T(4,128)S(1)}, f32[6,4,128]{2,1,0:T(4,128)S(1)}, u32[]{:S(2)}, u32[]{:S(2)}) collective-permute-start(f32[6,4,128]{2,1,0:T(4,128)S(1)} %get-tuple-element.32), channel_id=1, source_target_pairs={{1,0},{2,1},{3,2},{4,3},{5,4},{6,5},{7,6},{8,7},{9,8},{10,9},{11,1... | collective-permute-start | bytes 36872 | tf_op jit(solution)/shard_map/ppermute | solution.py:369
  15.8 13.3 %collective-permute-start = (f32[6,32,128]{2,1,0:T(8,128)S(1)}, f32[6,32,128]{2,1,0:T(8,128)S(1)}, u32[]{:S(2)}, u32[]{:S(2)}) collective-permute-start(f32[6,32,128]{2,1,0:T(8,128)S(1)} %get-tuple-element.29), channel_id=1, source_target_pairs={{0,32},{32,64},{64,96},{96,128},{128,160},{160,192},{192,224},{224... | collective-permute-start | bytes 294920 | tf_op jit(solution)/shard_map/ppermute | solution.py:368
  19.9 9.3 %collective-permute-start.1 = (f32[6,32,128]{2,1,0:T(8,128)S(1)}, f32[6,32,128]{2,1,0:T(8,128)S(1)}, u32[]{:S(2)}, u32[]{:S(2)}) collective-permute-start(f32[6,32,128]{2,1,0:T(8,128)S(1)} %get-tuple-element.30), channel_id=1, source_target_pairs={{32,0},{64,32},{96,64},{128,96},{160,128},{192,160},{224,192},{256... | collective-permute-start | bytes 294920 | tf_op jit(solution)/shard_map/ppermute | solution.py:369
  22.4 0.7 %copy-start.1 = (s32[1,1,128]{2,1,0:T(1,128)S(1)}, s32[1,1,128]{2,1,0:T(1,128)}, u32[]{:S(2)}) copy-start(s32[1,1,128]{2,1,0:T(1,128)} %param.17) | copy-start | bytes 1540
  35.3 9.0 %copy-start = (s32[1,1,16,128]{3,2,1,0:T(8,128)S(1)}, s32[1,1,16,128]{3,2,1,0:T(8,128)}, u32[]{:S(2)}) copy-start(s32[1,1,16,128]{3,2,1,0:T(8,128)} %param.21) | copy-start | bytes 24580
  35.3 16.8 %all-to-all-start = ((f32[16,6,128]{2,1,0:T(8,128)}), f32[16,6,128]{2,1,0:T(8,128)S(1)}, u32[]{:S(2)}, u32[]{:S(2)}) async-start(f32[16,6,128]{2,1,0:T(8,128)} %get-tuple-element.45), calls=%async_computation | async-start | bytes 131072 | tf_op jit(solution)/shard_map/all_to_all | solution.py:472

commit v3 on v2

--- a/solution.py
+++ b/solution.py
@@ -13,7 +13,7 @@
 LANES = 128
 INNER = 64
 RIM = 72
-NOWHERE = 255
+HALF = 32
 BY_MATRIX = 4
 STEPS = 1048000.0
 
@@ -46,12 +46,12 @@
     return correction
 
 
-def fill_table(table, rows, field, first, values):
+def fill_table(table, first, half, values):
     high = values.astype(jnp.bfloat16)
     low = (values - high.astype(jnp.float32)).astype(jnp.bfloat16)
-    count = values.shape[0]
-    table[field * rows + first : field * rows + first + count, 0:LANES] = high
-    table[field * rows + first : field * rows + first + count, LANES : 2 * LANES] = low
+    rows = slice(first, first + values.shape[0])
+    table[rows, half * LANES : (half + 1) * LANES] = high
+    table[rows, (half + 2) * LANES : (half + 3) * LANES] = low
 
 
 def fill_words(words, scales, corrected):
@@ -75,8 +75,7 @@
     cell = jnp.broadcast_to(cell, (8, LANES))
     pos = cell & (LANES - 1)
     line = (cell >> 7) - below
-    here = ((line & 7) == 0) & (line < rows) & (line >= 0)
-    share = jnp.where(here, jnp.broadcast_to(share, (8, LANES)), 0.0)
+    share = jnp.where((line & 7) == 0, jnp.broadcast_to(share, (8, LANES)), 0.0)
     hit = [None] * 4
     for first in range(0, rows, 8):
         chosen = line == first
@@ -99,21 +98,27 @@
 
 
 def gather(table, words, scales, rows, cells, shares, number):
-    at_cell = small(lax.broadcasted_iota(jnp.int32, (LANES, 2 * LANES), 0))
-    at_line = lax.broadcasted_iota(jnp.int32, (rows, 2 * LANES), 0)
+    at_cell = small(lax.broadcasted_iota(jnp.int32, (2 * LANES, 2 * LANES), 0))
+    at_line = lax.broadcasted_iota(jnp.int32, (rows - HALF, 2 * LANES), 0)
     one, zero = jnp.bfloat16(1), jnp.bfloat16(0)
+    extra = rows - 2 * HALF
     total = [None] * FIELDS
     for k in range(0, BY_MATRIX, 2):
         cell = jnp.concatenate([cells[k + i, pl.ds(number, 1), :] for i in (0, 1)], axis=1)
         share = jnp.concatenate([shares[k + i, pl.ds(number, 1), :] for i in (0, 1)], axis=1)
-        pick = jnp.where(at_cell == small(cell & (LANES - 1)), one, zero)
+        column = ((cell >> 5) & LANES) + (cell & (LANES - 1))
+        line = ((cell >> 7) & (HALF - 1)) + ((cell >> 8) & HALF)
+        pick = jnp.where(at_cell == small(column), one, zero)
         found = jnp.dot(
             table[...], jnp.concatenate([pick, pick], axis=0), preferred_element_type=jnp.float32
         )
-        weight = jnp.where(at_line == (cell >> 7), share, 0.0)
-        for f in range(FIELDS):
-            part = found[f * rows : (f + 1) * rows] * weight
-            part = jnp.sum(part.reshape(rows // 8, 8, 2 * LANES), axis=0)
+        weight = jnp.where(at_line == line, share, 0.0)
+        for f in range(FIELDS):
+            part = found[f * HALF : (f + 1) * HALF] * weight[:HALF]
+            part = jnp.sum(part.reshape(HALF // 8, 8, 2 * LANES), axis=0)
+            if extra:
+                first = FIELDS * HALF + f * extra
+                part = part + found[first : first + extra] * weight[HALF:]
             total[f] = part if k == 0 else total[f] + part
     by_lane = None
     for k in range(BY_MATRIX, DONORS):
@@ -128,20 +133,42 @@
     ]
 
 
+def prepare(receptor, lines, pick, taken):
+    at_line = lax.broadcasted_iota(jnp.int32, (INNER, LANES), 0)
+    at_cell = lax.broadcasted_iota(jnp.int32, (LANES, LANES), 1)
+    for number in range(receptor.shape[0]):
+        cell = receptor[number : number + 1, :]
+        line = cell >> 7
+        where = ((line >> 6) << 7) + (cell & (LANES - 1))
+        span = slice(number * LANES, (number + 1) * LANES)
+        lines[:, span] = jnp.where(at_line == (line & (INNER - 1)), 1.0, 0.0).astype(jnp.bfloat16)
+        where = jnp.transpose(jnp.broadcast_to(where, (LANES, LANES)))
+        for half in (0, 1):
+            pick[span, half * LANES : (half + 1) * LANES] = jnp.where(
+                at_cell + half * LANES == where, 1.0, 0.0
+            ).astype(jnp.bfloat16)
+    taken[...] = jnp.dot(lines[...], pick[...], preferred_element_type=jnp.float32)
+
+
 def load_kernel(
-    jac_in, coupling_in, inverse_in, flow_in, source_in, diag_in, cells_in, weights_in,
-    x_head, x_tail, y_head, y_tail, flow, source, diag, cells, weights, matrices,
-    jac, coupling, inverse, done,
+    jac_in, coupling_in, inverse_in, units_in, order_in, receptor_in,
+    flow_in, source_in, diag_in, cells_in, weights_in,
+    x_head, x_tail, y_head, y_tail, flow, source, diag, cells, weights,
+    live, lines, pick, taken, matrices,
+    jac, coupling, inverse, units, order, receptor, done,
 ):
     width_x, _, width_y, _ = flow.shape
     copies = [
         pltpu.make_async_copy(origin, target, done.at[number])
         for number, (origin, target) in enumerate(
             (
-                (flow_in, flow),
                 (jac_in, jac),
                 (coupling_in, coupling),
                 (inverse_in, inverse),
+                (units_in, units),
+                (order_in, order),
+                (receptor_in, receptor),
+                (flow_in, flow),
                 (flow_in.at[0], x_head),
                 (flow_in.at[width_x - 1], x_tail),
                 (source_in, source),
@@ -153,7 +180,7 @@
     ]
     for copy in copies:
         copy.start()
-    for copy in copies[1:4]:
+    for copy in copies[:6]:
         copy.wait()
     for f in range(FIELDS):
         for g in range(FIELDS):
@@ -166,28 +193,29 @@
                 for h in range(1, FIELDS):
                     total = total + inverse[f, h] * coupling[h, side, g]
                 matrices[1 + side, f, g] = total
-    copies[0].wait()
-    for f in range(FIELDS):
-        for x in range(width_x):
-            y_head[f, x : x + 1] = flow[x, f, 0:1]
-            y_tail[f, x : x + 1] = flow[x, f, width_y - 1 : width_y]
-    for copy in copies[4:]:
-        copy.wait()
-
-
-def inner_kernel(
-    matrices, units, flow, source, diag, order, cells, weights,
-    values, near, rim_residual, rim_scale, rim_live, rim_flow, rim_cells, shares,
-    live, inner_cells, table, words, scales,
-):
-    width_y = flow.shape[2]
-    blocks = cells.shape[1]
     line = lax.broadcasted_iota(jnp.int32, (LANES, LANES), 0)
     place = lax.broadcasted_iota(jnp.int32, (LANES, LANES), 1)
     hit = (line == order[...]) & (place < units[0, 0] * 32)
     live[...] = jnp.broadcast_to(
         jnp.max(jnp.where(hit, 1.0, 0.0), axis=1, keepdims=True), (LANES, LANES)
     )
+    prepare(receptor, lines, pick, taken)
+    copies[6].wait()
+    for f in range(FIELDS):
+        for x in range(width_x):
+            y_head[f, x : x + 1] = flow[x, f, 0:1]
+            y_tail[f, x : x + 1] = flow[x, f, width_y - 1 : width_y]
+    for copy in copies[7:]:
+        copy.wait()
+
+
+def inner_kernel(
+    matrices, flow, source, diag, live, cells, weights,
+    values, near, rim_residual, rim_scale, rim_live, rim_flow, rim_cells, rim_shares,
+    inner_cells, inner_shares, table, words, scales,
+):
+    width_y = flow.shape[2]
+    blocks = cells.shape[1]
     row = lax.broadcasted_iota(jnp.int32, (width_y, LANES), 0)
 
     cell = cells[...]
@@ -196,12 +224,15 @@
     middle = (x == 1) | (x == 2)
     edge = middle & ((y == 0) | (y == width_y - 1))
     pos = cell & (LANES - 1)
-    inner_cells[...] = (jnp.where(middle & ~edge, at - 32, NOWHERE) << 7) + pos
+    inner = middle & ~edge
+    inner_cells[...] = (((at - 32) & (INNER - 1)) << 7) + pos
     on_edge = 64 + (x - 1) + jnp.where(y == 0, 0, 2)
-    on_rim = jnp.where(x == 0, at, jnp.where(x == 3, at - 64, NOWHERE))
+    on_rim = jnp.where(x == 0, at, (at - 64) & 63)
     rim_cells[...] = (jnp.where(edge, on_edge, on_rim) << 7) + pos
     weight = weights[...]
-    shares[...] = weight / jnp.sum(weight, axis=0, keepdims=True)
+    share = weight / jnp.sum(weight, axis=0, keepdims=True)
+    inner_shares[...] = jnp.where(inner, share, 0.0)
+    rim_shares[...] = jnp.where(inner, 0.0, share)
 
     def residual_of(plane):
         total = [source[plane, f] for f in range(FIELDS)]
@@ -247,15 +278,15 @@
         for f in range(FIELDS):
             corrected = flow[plane, f] + jnp.where(alive > 0.5, correction[f], 0.0)
             near[number, f] = corrected
-            fill_table(table, INNER, f, number * width_y, corrected)
+            fill_table(table, f * HALF, number, corrected)
 
     fill_words(
         words, scales, lambda f: jnp.concatenate([near[0, f], near[1, f]], axis=0)
     )
 
-    @pl.loop(0, blocks, unroll=4)
+    @pl.loop(0, blocks, unroll=8)
     def _(number):
-        found = gather(table, words, scales, INNER, inner_cells, shares, number)
+        found = gather(table, words, scales, INNER, inner_cells, inner_shares, number)
         for f in range(FIELDS):
             values[number, f : f + 1, :] = found[f]
 
@@ -285,8 +316,8 @@
                 )
     for f in range(FIELDS):
         residual[f, RIM - 4 : RIM] = jnp.zeros((4, LANES), jnp.float32)
-    for first in range(0, RIM, 24):
-        rows = slice(first, first + 24)
+    edges = []
+    for half, rows in enumerate((slice(0, 32), slice(32, 64), slice(64, RIM))):
         correction = solve(
             [residual[f, rows] for f in range(FIELDS)], rim_scale[rows], matrices
         )
@@ -294,52 +325,25 @@
         for f in range(FIELDS):
             corrected = rim_flow[f, rows] + jnp.where(alive, correction[f], 0.0)
             rim[f, rows] = corrected
-            fill_table(table, RIM, f, first, corrected)
-
+            if half < 2:
+                fill_table(table, f * HALF, half, corrected)
+            else:
+                edges.append(corrected)
+    edges = jnp.concatenate(edges, axis=0)
+    fill_table(table, FIELDS * HALF, 0, edges)
+    fill_table(table, FIELDS * HALF, 1, jnp.zeros_like(edges))
     fill_words(words, scales, lambda f: rim[f])
 
-    @pl.loop(0, blocks, unroll=4)
+    @pl.loop(0, blocks, unroll=8)
     def _(number):
         found = gather(table, words, scales, RIM, rim_cells, shares, number)
         for f in range(FIELDS):
             values[number, f : f + 1, :] = found[f] + part[number, f : f + 1, :]
 
 
-def prepare_kernel(receptor, near, rim, base, lines, pick):
-    blocks = receptor.shape[0]
+def place_kernel(incoming, near, rim, lines, pick, taken, updated, high, low):
+    blocks = incoming.shape[0]
     width_y = near.shape[2]
-    at_line = lax.broadcasted_iota(jnp.int32, (INNER, LANES), 0)
-    at_cell = lax.broadcasted_iota(jnp.int32, (LANES, LANES), 1)
-    for number in range(blocks):
-        cell = receptor[number : number + 1, :]
-        line = cell >> 7
-        where = ((line >> 6) << 7) + (cell & (LANES - 1))
-        span = slice(number * LANES, (number + 1) * LANES)
-        lines[:, span] = jnp.where(at_line == (line & (INNER - 1)), 1.0, 0.0).astype(jnp.bfloat16)
-        where = jnp.transpose(jnp.broadcast_to(where, (LANES, LANES)))
-        for half in (0, 1):
-            pick[span, half * LANES : (half + 1) * LANES] = jnp.where(
-                at_cell + half * LANES == where, 1.0, 0.0
-            ).astype(jnp.bfloat16)
-    taken = jnp.dot(lines[...], pick[...], preferred_element_type=jnp.float32)
-    for plane in range(4):
-        rows = (plane % 2) * width_y
-        lanes = slice((plane // 2) * LANES, (plane // 2 + 1) * LANES)
-        free = taken[rows : rows + width_y, lanes] < 0.5
-        for f in range(FIELDS):
-            if plane in (0, 3):
-                at_row = 0 if plane == 0 else width_y
-                base[plane, f] = jnp.where(free, rim[f, at_row : at_row + width_y], 0.0)
-                continue
-            base[plane, f] = jnp.where(free, near[plane - 1, f], 0.0)
-            for at_row, y_line in ((63 + plane, 0), (65 + plane, width_y - 1)):
-                one = slice(y_line, y_line + 1)
-                base[plane, f, one] = jnp.where(free[one], rim[f, at_row : at_row + 1], 0.0)
-
-
-def place_kernel(incoming, base, lines, pick, updated, high, low):
-    blocks = incoming.shape[0]
-    width_y = base.shape[2]
     for number in range(blocks):
         span = slice(number * LANES, (number + 1) * LANES)
         value = incoming[number]
@@ -357,10 +361,19 @@
     for plane in range(4):
         rows = (plane % 2) * width_y
         lanes = slice((plane // 2) * LANES, (plane // 2 + 1) * LANES)
-        for f in range(FIELDS):
-            updated[plane, f] = (
-                base[plane, f] + placed[f * INNER + rows : f * INNER + rows + width_y, lanes]
-            )
+        free = taken[rows : rows + width_y, lanes] < 0.5
+        for f in range(FIELDS):
+            value = placed[f * INNER + rows : f * INNER + rows + width_y, lanes]
+            if plane in (0, 3):
+                at_row = 0 if plane == 0 else width_y
+                updated[plane, f] = jnp.where(free, rim[f, at_row : at_row + width_y], value)
+                continue
+            updated[plane, f] = jnp.where(free, near[plane - 1, f], value)
+            for at_row, y_line in ((63 + plane, 0), (65 + plane, width_y - 1)):
+                one = slice(y_line, y_line + 1)
+                updated[plane, f, one] = jnp.where(
+                    free[one], rim[f, at_row : at_row + 1], value[one]
+                )
 
 
 def halo(ends, axis, head, tail):
@@ -400,26 +413,39 @@
 
     outside = pl.BlockSpec(memory_space=pltpu.HBM)
     raw = [
-        pltpu.with_memory_space_constraint(array, pltpu.HBM)
-        for array in (jac, coupling, block_inverse, flow, source, diag_scale, cells, weights)
+        array if array is active_units else pltpu.with_memory_space_constraint(array, pltpu.HBM)
+        for array in (
+            jac, coupling, block_inverse, active_units, active_order.reshape(1, LANES),
+            receptor, flow, source, diag_scale, cells, weights,
+        )
     ]
-    x_head, x_tail, y_head, y_tail, flow, source, diag, cells, weights, matrices = pl.pallas_call(
+    *edges, flow, source, diag, cells, weights, live, lines, pick, taken, matrices = pl.pallas_call(
         load_kernel,
         out_shape=[like((fields, width_y, length), f32)] * 2
         + [like((fields, width_x, length), f32)] * 2
-        + [like(array.shape, array.dtype) for array in raw[3:]]
-        + [like((8, fields, fields), f32)],
-        in_specs=[outside] * 8,
-        out_specs=[vmem] * 9 + [smem],
+        + [like(array.shape, array.dtype) for array in raw[6:]]
+        + [
+            like((LANES, LANES), f32),
+            like((INNER, blocks * LANES), jnp.bfloat16),
+            like((blocks * LANES, 2 * LANES), jnp.bfloat16),
+            like((INNER, 2 * LANES), f32),
+            like((8, fields, fields), f32),
+        ],
+        in_specs=[outside] * 11,
+        out_specs=[vmem] * 13 + [smem],
         scratch_shapes=[
             pltpu.SMEM(jac.shape, f32),
             pltpu.SMEM(coupling.shape, f32),
             pltpu.SMEM(block_inverse.shape, f32),
-            pltpu.SemaphoreType.DMA((10,)),
+            pltpu.SMEM(active_units.shape, i32),
+            pltpu.VMEM((1, LANES), i32),
+            pltpu.VMEM(receptor.shape, i32),
+            pltpu.SemaphoreType.DMA((13,)),
         ],
         compiler_params=params,
         name="load_block",
     )(*raw)
+    x_head, x_tail, y_head, y_tail = edges
     x_prev, x_next = halo(lax.axis_size("blk") - 1, "blk", x_head, x_tail)
     y_prev, y_next = halo(lax.axis_size("bal") - 1, "bal", y_head, y_tail)
     part, near, *rest = pl.pallas_call(
@@ -434,12 +460,12 @@
             like(cells.shape, i32),
             like(cells.shape, f32),
         ],
-        in_specs=[smem] * 2 + [vmem] * 6,
+        in_specs=[smem] + [vmem] * 6,
         out_specs=[vmem] * 8,
         scratch_shapes=[
-            pltpu.VMEM((LANES, LANES), f32),
             pltpu.VMEM(cells.shape, i32),
-            pltpu.VMEM((fields * INNER, 2 * LANES), jnp.bfloat16),
+            pltpu.VMEM(cells.shape, f32),
+            pltpu.VMEM((fields * HALF, 4 * LANES), jnp.bfloat16),
             pltpu.VMEM((4, INNER, LANES), i32),
             pltpu.VMEM((fields, 8, LANES), f32),
         ],
@@ -449,8 +475,7 @@
         compiler_params=params,
         name="inner_lines",
     )(
-        matrices, active_units, flow, source, diag,
-        active_order.reshape(1, LANES), cells, weights,
+        matrices, flow, source, diag, live, cells, weights,
     )
     values, rim = pl.pallas_call(
         rim_kernel,
@@ -462,7 +487,7 @@
         out_specs=[vmem] * 2,
         scratch_shapes=[
             pltpu.VMEM((fields, RIM, length), f32),
-            pltpu.VMEM((fields * RIM, 2 * LANES), jnp.bfloat16),
+            pltpu.VMEM((fields * (RIM - HALF), 4 * LANES), jnp.bfloat16),
             pltpu.VMEM((4, RIM, LANES), i32),
             pltpu.VMEM((fields, 8, LANES), f32),
         ],
@@ -470,30 +495,15 @@
         name="rim_lines",
     )(matrices, x_prev, x_next, y_prev, y_next, part, *rest)
     incoming = lax.all_to_all(values, "blk", split_axis=0, concat_axis=0, tiled=True)
-    base, lines, pick = pl.pallas_call(
-        prepare_kernel,
-        out_shape=[
-            like(flow.shape, f32),
-            like((INNER, blocks * LANES), jnp.bfloat16),
-            like((blocks * LANES, 2 * LANES), jnp.bfloat16),
-        ],
-        in_specs=[vmem] * 3,
-        out_specs=[vmem] * 3,
-        cost_estimate=pl.CostEstimate(
-            flops=5 * 10**9, bytes_accessed=3 * 10**6, transcendentals=0
-        ),
-        compiler_params=params,
-        name="prepare_receptors",
-    )(receptor, near, rim)
     updated = pl.pallas_call(
         place_kernel,
         out_shape=like(flow.shape, f32),
-        in_specs=[vmem] * 4,
+        in_specs=[vmem] * 6,
         out_specs=vmem,
         scratch_shapes=[pltpu.VMEM((fields * INNER, blocks * LANES), jnp.bfloat16)] * 2,
         compiler_params=params,
         name="place_receptors",
-    )(incoming, base, lines, pick)
+    )(incoming, near, rim, lines, pick, taken)
     return jnp.transpose(updated, (0, 2, 1, 3))
 
 

time: 54.3 us -> 52.5 us (0.967)
  blocking collectives: 0 us -> 16.5 us
  starting transfers between devices: 27.8 us -> 18.8 us
  waiting for transfers between devices: 7.17 us -> 0.01 us
  Pallas kernels: 17.6 us -> 16.1 us
  local copies, waits for them, and re-layouts: 0.65 us -> 0 us
    all_to_all x0 -> x1, blocking collectives: none -> 16.5 us  [shards(): lax.all_to_all(values, 'blk', split_axis=0, concat_axis=0, tiled=True)]
    all_to_all x1 -> x0, starting transfers between devices: 9.03 us -> none  [shards(): lax.all_to_all(values, 'blk', split_axis=0, concat_axis=0, tiled=True)]
    all_to_all x1 -> x0, waiting for transfers between devices: 7.16 us -> none  [shards(): lax.all_to_all(values, 'blk', split_axis=0, concat_axis=0, tiled=True)]
    pallas_call x1, Pallas kernels: 6.18 us -> 5.32 us  [shards(): pl.pallas_call(rim_kernel, out_shape=[like((blocks, fields, length), f32)...]
    unnamed x4 -> x0, local copies, waits for them, and re-layouts: 0.65 us -> none
    pallas_call x1 -> x0, Pallas kernels: 0.64 us -> none  [shards(): pl.pallas_call(prepare_kernel, out_shape=[like(flow.shape, f32), like((IN...]
  transfers between devices with their start and end apart: 5 -> 4, of which waited for: 1 -> 0; matrix products, arithmetic and copies ran while one was open for 0% -> 0% of each run, Pallas kernels for 12% -> 11%
where the time goes in v3:
time: 52.5 us; the launch traced here: 52.1 us
  starting transfers between devices  18.8 us (36%)
  blocking collectives  16.5 us (31%)
  Pallas kernels  16.1 us (31%)
  between operations  0.73 us (1%)
    all_to_all x1, blocking collectives, shards(): lax.all_to_all(values, 'blk', split_axis=0, concat_axis=0, tiled=True)  16.5 us
    ppermute x2, starting transfers between devices, halo(): lax.ppermute(head, axis, [(i + 1, i) for i in range(ends)])  10.8 us
    ppermute x2, starting transfers between devices, halo(): lax.ppermute(tail, axis, [(i, i + 1) for i in range(ends)])  8.05 us
    pallas_call x1, Pallas kernels, shards(): pl.pallas_call(inner_kernel, out_shape=[like((blocks, fields, length), f3...  5.91 us
    pallas_call x1, Pallas kernels, shards(): pl.pallas_call(rim_kernel, out_shape=[like((blocks, fields, length), f32)...  5.32 us
    pallas_call x1, Pallas kernels, shards(): pl.pallas_call(load_kernel, out_shape=[like((fields, width_y, length), f3...  3.06 us
    pallas_call x1, Pallas kernels, shards(): pl.pallas_call(place_kernel, out_shape=like(flow.shape, f32), in_specs=[v...  1.81 us
  transfers between devices with their start and end apart: 4, of which 0 were waited for; matrix products, arithmetic and copies ran while one was open for 0% of the time, Pallas kernels for 11%

profile of v3, /device:TPU:7, one launch (start us, length us, event | category | flops | bytes accessed | tf_op | source)
XLA Modules:
  0.0 52.1 jit_solution(8925330430040050010)
XLA Ops:
  0.7 3.1 %load_block.1 = (f32[6,32,128]{2,1,0:T(8,128)S(1)}, f32[6,32,128]{2,1,0:T(8,128)S(1)}, f32[6,4,128]{2,1,0:T(4,128)S(1)}, f32[6,4,128]{2,1,0:T(4,128)S(1)}, f32[4...) custom-call(f32[6,4,6]{2,1,0:T(4,128)} %bitcast.13, ...), custom_call_target="tpu_custom_call" | custom-call | tf_op jit(solution)/shard_map/load_block/pallas_call | solution.py:422
  3.7 4.0 %collective-permute-start.2 = (f32[6,4,128]{2,1,0:T(4,128)S(1)}, f32[6,4,128]{2,1,0:T(4,128)S(1)}, u32[]{:S(2)}, u32[]{:S(2)}) collective-permute-start(f32[6,4,128]{2,1,0:T(4,128)S(1)} %get-tuple-element.32), channel_id=1, source_target_pairs={{0,1},{1,2},{2,3},{3,4},{4,5},{5,6},{6,7},{7,8},{8,9},{9,10},{10,1... | collective-permute-start | bytes 36872 | tf_op jit(solution)/shard_map/ppermute | solution.py:381
  7.7 8.9 %collective-permute-start.3 = (f32[6,4,128]{2,1,0:T(4,128)S(1)}, f32[6,4,128]{2,1,0:T(4,128)S(1)}, u32[]{:S(2)}, u32[]{:S(2)}) collective-permute-start(f32[6,4,128]{2,1,0:T(4,128)S(1)} %get-tuple-element.33), channel_id=1, source_target_pairs={{1,0},{2,1},{3,2},{4,3},{5,4},{6,5},{7,6},{8,7},{9,8},{10,9},{11,1... | collective-permute-start | bytes 36872 | tf_op jit(solution)/shard_map/ppermute | solution.py:382
  16.6 4.0 %collective-permute-start = (f32[6,32,128]{2,1,0:T(8,128)S(1)}, f32[6,32,128]{2,1,0:T(8,128)S(1)}, u32[]{:S(2)}, u32[]{:S(2)}) collective-permute-start(f32[6,32,128]{2,1,0:T(8,128)S(1)} %get-tuple-element.30), channel_id=1, source_target_pairs={{0,32},{32,64},{64,96},{96,128},{128,160},{160,192},{192,224},{224... | collective-permute-start | bytes 294920 | tf_op jit(solution)/shard_map/ppermute | solution.py:381
  20.6 1.9 %collective-permute-start.1 = (f32[6,32,128]{2,1,0:T(8,128)S(1)}, f32[6,32,128]{2,1,0:T(8,128)S(1)}, u32[]{:S(2)}, u32[]{:S(2)}) collective-permute-start(f32[6,32,128]{2,1,0:T(8,128)S(1)} %get-tuple-element.31), channel_id=1, source_target_pairs={{32,0},{64,32},{96,64},{128,96},{160,128},{192,160},{224,192},{256... | collective-permute-start | bytes 294920 | tf_op jit(solution)/shard_map/ppermute | solution.py:382
  22.6 5.9 %inner_lines.1 = (f32[16,6,128]{2,1,0:T(8,128)S(1)}, f32[2,6,32,128]{3,2,1,0:T(8,128)S(1)}, f32[6,72,128]{2,1,0:T(8,128)S(1)}, f32[72,128]{1,0:T(8,128)S(1)}, f3...) custom-call(f32[8,6,6]{2,1,0:T(8,128)S(1)} %get-tuple-element.29.matrice, ...), custom_call_target="tpu_custom_call" | custom-call | flops 10000000000 | bytes 3000000 | tf_op jit(solution)/shard_map/inner_lines/pallas_call | solution.py:451
  28.5 0.0 collective-permute-done.2.y_prev
  28.5 0.0 collective-permute-done.3.y_next
  28.5 0.0 collective-permute-done.x_prev
  28.5 0.0 collective-permute-done.1.x_next
  28.5 5.3 %rim_lines.1 = (f32[16,6,128]{2,1,0:T(8,128)S(1)}, f32[6,72,128]{2,1,0:T(8,128)S(1)}) custom-call(f32[8,6,6]{2,1,0:T(8,128)S(1)} %get-tuple-element.29.matrices, f32[6,32,128]{2,1,0:T(8,128)S(1)} %collective-permute-done.x_prev, f32[6,32,128]{2,1,0:T(8,128)S(1)} %collective-permute-done.1.x_next, f32[6,4,128]{2,1,0:T(4,128)S(1)} %collective-permute-done.2.y_prev, ...), custom_call_target="tpu_custom_call" | custom-call | tf_op jit(solution)/shard_map/rim_lines/pallas_call | solution.py:480
  33.9 16.5 %all_to_all.5.incoming = f32[16,6,128]{2,1,0:T(8,128)S(1)} all-to-all(f32[16,6,128]{2,1,0:T(8,128)S(1)} %get-tuple-element.47), channel_id=1, replica_groups=mesh['blk'=16,'bal'=32] {'blk'}, dimensions={0} | all-to-all | bytes 98304 | tf_op jit(solution)/shard_map/all_to_all | solution.py:497
  50.3 1.8 %place_receptors.1 = f32[4,6,32,128]{3,2,1,0:T(8,128)} custom-call(f32[16,6,128]{2,1,0:T(8,128)S(1)} %all_to_all.5.incoming, f32[2,6,32,128]{3,2,1,0:T(8,128)S(1)} %get-tuple-element.48.near, f32[6,72,128]{2,1,0:T(8,128)S(1)} %get-tuple-element.49.rim, bf16[64,2048]{1,0:T(8,128)(2,1)S(1)} %get-tuple-element.50.lines, ...), custom_call_target="tpu_custom_call" | custom-call | tf_op jit(solution)/shard_map/place_receptors/pallas_call | solution.py:498
Async XLA Ops:
  3.7 24.8 %collective-permute-start.2 = (f32[6,4,128]{2,1,0:T(4,128)S(1)}, f32[6,4,128]{2,1,0:T(4,128)S(1)}, u32[]{:S(2)}, u32[]{:S(2)}) collective-permute-start(f32[6,4,128]{2,1,0:T(4,128)S(1)} %get-tuple-element.32), channel_id=1, source_target_pairs={{0,1},{1,2},{2,3},{3,4},{4,5},{5,6},{6,7},{7,8},{8,9},{9,10},{10,1... | collective-permute-start | bytes 36872 | tf_op jit(solution)/shard_map/ppermute | solution.py:381
  7.7 20.8 %collective-permute-start.3 = (f32[6,4,128]{2,1,0:T(4,128)S(1)}, f32[6,4,128]{2,1,0:T(4,128)S(1)}, u32[]{:S(2)}, u32[]{:S(2)}) collective-permute-start(f32[6,4,128]{2,1,0:T(4,128)S(1)} %get-tuple-element.33), channel_id=1, source_target_pairs={{1,0},{2,1},{3,2},{4,3},{5,4},{6,5},{7,6},{8,7},{9,8},{10,9},{11,1... | collective-permute-start | bytes 36872 | tf_op jit(solution)/shard_map/ppermute | solution.py:382
  16.6 11.9 %collective-permute-start = (f32[6,32,128]{2,1,0:T(8,128)S(1)}, f32[6,32,128]{2,1,0:T(8,128)S(1)}, u32[]{:S(2)}, u32[]{:S(2)}) collective-permute-start(f32[6,32,128]{2,1,0:T(8,128)S(1)} %get-tuple-element.30), channel_id=1, source_target_pairs={{0,32},{32,64},{64,96},{96,128},{128,160},{160,192},{192,224},{224... | collective-permute-start | bytes 294920 | tf_op jit(solution)/shard_map/ppermute | solution.py:381
  20.6 7.9 %collective-permute-start.1 = (f32[6,32,128]{2,1,0:T(8,128)S(1)}, f32[6,32,128]{2,1,0:T(8,128)S(1)}, u32[]{:S(2)}, u32[]{:S(2)}) collective-permute-start(f32[6,32,128]{2,1,0:T(8,128)S(1)} %get-tuple-element.31), channel_id=1, source_target_pairs={{32,0},{64,32},{96,64},{128,96},{160,128},{192,160},{224,192},{256... | collective-permute-start | bytes 294920 | tf_op jit(solution)/shard_map/ppermute | solution.py:382

commit v4 on v3

--- a/solution.py
+++ b/solution.py
@@ -18,6 +18,11 @@
 STEPS = 1048000.0
 
 
+def entry(number, f, g):
+    row = (number * FIELDS + f) * FIELDS + g
+    return slice(row, row + 1)
+
+
 def apply(matrix, values):
     out = []
     for f in range(FIELDS):
@@ -31,7 +36,7 @@
 def solve(residual, scale_inv, matrices):
     lane = lax.broadcasted_iota(jnp.int32, residual[0].shape, 1)
     first, last = lane == 0, lane == LANES - 1
-    base = apply(lambda f, g: matrices[3, f, g], residual)
+    base = apply(lambda f, g: matrices[entry(3, f, g)], residual)
     base = [value * scale_inv for value in base]
     correction = base
     for _ in range(SWEEPS - 1):
@@ -40,7 +45,7 @@
             down = jnp.where(first, 0.0, pltpu.roll(correction[g], 1, 1))
             up = jnp.where(last, 0.0, pltpu.roll(correction[g], LANES - 1, 1))
             for f in range(FIELDS):
-                term = matrices[1, f, g] * down + matrices[2, f, g] * up
+                term = matrices[entry(1, f, g)] * down + matrices[entry(2, f, g)] * up
                 total[f] = term if g == 0 else total[f] + term
         correction = [base[f] - scale_inv * total[f] for f in range(FIELDS)]
     return correction
@@ -184,15 +189,16 @@
         copy.wait()
     for f in range(FIELDS):
         for g in range(FIELDS):
-            for side in range(4):
-                matrices[4 + side, f, g] = jac[f, side, g]
-            matrices[0, f, g] = jac[f, 0, g] + jac[f, 1, g] + jac[f, 2, g] + jac[f, 3, g]
-            matrices[3, f, g] = inverse[f, g]
+            values = [jac[f, 0, g] + jac[f, 1, g] + jac[f, 2, g] + jac[f, 3, g]]
             for side in (0, 1):
                 total = inverse[f, 0] * coupling[0, side, g]
                 for h in range(1, FIELDS):
                     total = total + inverse[f, h] * coupling[h, side, g]
-                matrices[1 + side, f, g] = total
+                values.append(total)
+            values.append(inverse[f, g])
+            values += [jac[f, side, g] for side in range(4)]
+            for number, value in enumerate(values):
+                matrices[entry(number, f, g)] = jnp.full((1, LANES), value, jnp.float32)
     line = lax.broadcasted_iota(jnp.int32, (LANES, LANES), 0)
     place = lax.broadcasted_iota(jnp.int32, (LANES, LANES), 1)
     hit = (line == order[...]) & (place < units[0, 0] * 32)
@@ -243,12 +249,12 @@
             before = jnp.where(row == 0, 0.0, pltpu.roll(here, 1, 0))
             after = jnp.where(row == width_y - 1, 0.0, pltpu.roll(here, width_y - 1, 0))
             for f in range(FIELDS):
-                value = total[f] - matrices[0, f, g] * here
+                value = total[f] - matrices[entry(0, f, g)] * here
                 if left is not None:
-                    value = value + matrices[4, f, g] * left
+                    value = value + matrices[entry(4, f, g)] * left
                 if right is not None:
-                    value = value + matrices[5, f, g] * right
-                total[f] = value + matrices[6, f, g] * before + matrices[7, f, g] * after
+                    value = value + matrices[entry(5, f, g)] * right
+                total[f] = value + matrices[entry(6, f, g)] * before + matrices[entry(7, f, g)] * after
         return total
 
     for number, plane in enumerate((0, 3)):
@@ -300,11 +306,11 @@
     blocks = rim_cells.shape[1]
     for number, (side, halo) in enumerate(((0, x_prev), (1, x_next))):
         rows = slice(number * width_y, (number + 1) * width_y)
-        added = apply(lambda f, g: matrices[4 + side, f, g], [halo[g] for g in range(FIELDS)])
+        added = apply(lambda f, g: matrices[entry(4 + side, f, g)], [halo[g] for g in range(FIELDS)])
         for f in range(FIELDS):
             residual[f, rows] = rim_residual[f, rows] + added[f]
     for number, (side, halo) in enumerate(((2, y_prev), (3, y_next))):
-        added = apply(lambda f, g: matrices[4 + side, f, g], [halo[g] for g in range(FIELDS)])
+        added = apply(lambda f, g: matrices[entry(4 + side, f, g)], [halo[g] for g in range(FIELDS)])
         for f in range(FIELDS):
             at_row = 64 + 2 * number
             residual[f, at_row : at_row + 2] = (
@@ -398,7 +404,6 @@
 ):
     f32, i32 = jnp.float32, jnp.int32
     vmem = pl.BlockSpec(memory_space=pltpu.VMEM)
-    smem = pl.BlockSpec(memory_space=pltpu.SMEM)
     like = jax.ShapeDtypeStruct
     params = pltpu.CompilerParams(vmem_limit_bytes=32 << 20)
     flow = jnp.transpose(flow_state, (0, 2, 1, 3))
@@ -429,10 +434,10 @@
             like((INNER, blocks * LANES), jnp.bfloat16),
             like((blocks * LANES, 2 * LANES), jnp.bfloat16),
             like((INNER, 2 * LANES), f32),
-            like((8, fields, fields), f32),
+            like((8 * fields * fields, length), f32),
         ],
         in_specs=[outside] * 11,
-        out_specs=[vmem] * 13 + [smem],
+        out_specs=[vmem] * 14,
         scratch_shapes=[
             pltpu.SMEM(jac.shape, f32),
             pltpu.SMEM(coupling.shape, f32),
@@ -460,7 +465,7 @@
             like(cells.shape, i32),
             like(cells.shape, f32),
         ],
-        in_specs=[smem] + [vmem] * 6,
+        in_specs=[vmem] * 7,
         out_specs=[vmem] * 8,
         scratch_shapes=[
             pltpu.VMEM(cells.shape, i32),
@@ -483,7 +488,7 @@
             like((blocks, fields, length), f32),
             like((fields, RIM, length), f32),
         ],
-        in_specs=[smem] + [vmem] * 11,
+        in_specs=[vmem] * 12,
         out_specs=[vmem] * 2,
         scratch_shapes=[
             pltpu.VMEM((fields, RIM, length), f32),

time: 52.5 us -> 49.1 us (0.935)
  Pallas kernels: 16.1 us -> 12.8 us
    pallas_call x1, Pallas kernels: 3.06 us -> 1.91 us  [shards(): pl.pallas_call(load_kernel, out_shape=[like((fields, width_y, length), f3...]
    pallas_call x1, Pallas kernels: 5.91 us -> 4.78 us  [shards(): pl.pallas_call(inner_kernel, out_shape=[like((blocks, fields, length), f3...]
    pallas_call x1, Pallas kernels: 5.32 us -> 4.32 us  [shards(): pl.pallas_call(rim_kernel, out_shape=[like((blocks, fields, length), f32)...]
  transfers between devices with their start and end apart: 4 -> 4, of which waited for: 0 -> 0; matrix products, arithmetic and copies ran while one was open for 0% -> 0% of each run, Pallas kernels for 11% -> 10%
where the time goes in v4:
time: 49.1 us; the launch traced here: 48.8 us
  starting transfers between devices  18.8 us (38%)
  blocking collectives  16.5 us (34%)
  Pallas kernels  12.8 us (26%)
  between operations  0.73 us (1%)
    all_to_all x1, blocking collectives, shards(): lax.all_to_all(values, 'blk', split_axis=0, concat_axis=0, tiled=True)  16.5 us
    ppermute x2, starting transfers between devices, halo(): lax.ppermute(head, axis, [(i + 1, i) for i in range(ends)])  10.8 us
    ppermute x2, starting transfers between devices, halo(): lax.ppermute(tail, axis, [(i, i + 1) for i in range(ends)])  8.05 us
    pallas_call x1, Pallas kernels, shards(): pl.pallas_call(inner_kernel, out_shape=[like((blocks, fields, length), f3...  4.78 us
    pallas_call x1, Pallas kernels, shards(): pl.pallas_call(rim_kernel, out_shape=[like((blocks, fields, length), f32)...  4.32 us
    pallas_call x1, Pallas kernels, shards(): pl.pallas_call(load_kernel, out_shape=[like((fields, width_y, length), f3...  1.91 us
    pallas_call x1, Pallas kernels, shards(): pl.pallas_call(place_kernel, out_shape=like(flow.shape, f32), in_specs=[v...  1.81 us
  transfers between devices with their start and end apart: 4, of which 0 were waited for; matrix products, arithmetic and copies ran while one was open for 0% of the time, Pallas kernels for 10%

profile of v4, /device:TPU:7, one launch (start us, length us, event | category | flops | bytes accessed | tf_op | source)
XLA Modules:
  0.0 48.8 jit_solution(9492367266791858710)
XLA Ops:
  0.7 1.9 %load_block.1 = (f32[6,32,128]{2,1,0:T(8,128)S(1)}, f32[6,32,128]{2,1,0:T(8,128)S(1)}, f32[6,4,128]{2,1,0:T(4,128)S(1)}, f32[6,4,128]{2,1,0:T(4,128)S(1)}, f32[4...) custom-call(f32[6,4,6]{2,1,0:T(4,128)} %bitcast.13, ...), custom_call_target="tpu_custom_call" | custom-call | tf_op jit(solution)/shard_map/load_block/pallas_call | solution.py:427
  2.6 4.0 %collective-permute-start.2 = (f32[6,4,128]{2,1,0:T(4,128)S(1)}, f32[6,4,128]{2,1,0:T(4,128)S(1)}, u32[]{:S(2)}, u32[]{:S(2)}) collective-permute-start(f32[6,4,128]{2,1,0:T(4,128)S(1)} %get-tuple-element.32), channel_id=1, source_target_pairs={{0,1},{1,2},{2,3},{3,4},{4,5},{5,6},{6,7},{7,8},{8,9},{9,10},{10,1... | collective-permute-start | bytes 36872 | tf_op jit(solution)/shard_map/ppermute | solution.py:387
  6.6 8.9 %collective-permute-start.3 = (f32[6,4,128]{2,1,0:T(4,128)S(1)}, f32[6,4,128]{2,1,0:T(4,128)S(1)}, u32[]{:S(2)}, u32[]{:S(2)}) collective-permute-start(f32[6,4,128]{2,1,0:T(4,128)S(1)} %get-tuple-element.33), channel_id=1, source_target_pairs={{1,0},{2,1},{3,2},{4,3},{5,4},{6,5},{7,6},{8,7},{9,8},{10,9},{11,1... | collective-permute-start | bytes 36872 | tf_op jit(solution)/shard_map/ppermute | solution.py:388
  15.4 4.0 %collective-permute-start = (f32[6,32,128]{2,1,0:T(8,128)S(1)}, f32[6,32,128]{2,1,0:T(8,128)S(1)}, u32[]{:S(2)}, u32[]{:S(2)}) collective-permute-start(f32[6,32,128]{2,1,0:T(8,128)S(1)} %get-tuple-element.30), channel_id=1, source_target_pairs={{0,32},{32,64},{64,96},{96,128},{128,160},{160,192},{192,224},{224... | collective-permute-start | bytes 294920 | tf_op jit(solution)/shard_map/ppermute | solution.py:387
  19.5 1.9 %collective-permute-start.1 = (f32[6,32,128]{2,1,0:T(8,128)S(1)}, f32[6,32,128]{2,1,0:T(8,128)S(1)}, u32[]{:S(2)}, u32[]{:S(2)}) collective-permute-start(f32[6,32,128]{2,1,0:T(8,128)S(1)} %get-tuple-element.31), channel_id=1, source_target_pairs={{32,0},{64,32},{96,64},{128,96},{160,128},{192,160},{224,192},{256... | collective-permute-start | bytes 294920 | tf_op jit(solution)/shard_map/ppermute | solution.py:388
  21.4 4.8 %inner_lines.1 = (f32[16,6,128]{2,1,0:T(8,128)S(1)}, f32[2,6,32,128]{3,2,1,0:T(8,128)S(1)}, f32[6,72,128]{2,1,0:T(8,128)S(1)}, f32[72,128]{1,0:T(8,128)S(1)}, f3...) custom-call(f32[288,128]{1,0:T(8,128)S(1)} %get-tuple-element.29.matrice, ...), custom_call_target="tpu_custom_call" | custom-call | flops 10000000000 | bytes 3000000 | tf_op jit(solution)/shard_map/inner_lines/pallas_call | solution.py:456
  26.2 0.0 collective-permute-done.2.y_prev
  26.2 0.0 collective-permute-done.3.y_next
  26.2 0.0 collective-permute-done.x_prev
  26.2 0.0 collective-permute-done.1.x_next
  26.2 4.3 %rim_lines.1 = (f32[16,6,128]{2,1,0:T(8,128)S(1)}, f32[6,72,128]{2,1,0:T(8,128)S(1)}) custom-call(f32[288,128]{1,0:T(8,128)S(1)} %get-tuple-element.29.matrices, f32[6,32,128]{2,1,0:T(8,128)S(1)} %collective-permute-done.x_prev, f32[6,32,128]{2,1,0:T(8,128)S(1)} %collective-permute-done.1.x_next, f32[6,4,128]{2,1,0:T(4,128)S(1)} %collective-permute-done.2.y_prev, ...), custom_call_target="tpu_custom_call" | custom-call | tf_op jit(solution)/shard_map/rim_lines/pallas_call | solution.py:485
  30.6 16.5 %all_to_all.5.incoming = f32[16,6,128]{2,1,0:T(8,128)S(1)} all-to-all(f32[16,6,128]{2,1,0:T(8,128)S(1)} %get-tuple-element.47), channel_id=1, replica_groups=mesh['blk'=16,'bal'=32] {'blk'}, dimensions={0} | all-to-all | bytes 98304 | tf_op jit(solution)/shard_map/all_to_all | solution.py:502
  47.0 1.8 %place_receptors.1 = f32[4,6,32,128]{3,2,1,0:T(8,128)} custom-call(f32[16,6,128]{2,1,0:T(8,128)S(1)} %all_to_all.5.incoming, f32[2,6,32,128]{3,2,1,0:T(8,128)S(1)} %get-tuple-element.48.near, f32[6,72,128]{2,1,0:T(8,128)S(1)} %get-tuple-element.49.rim, bf16[64,2048]{1,0:T(8,128)(2,1)S(1)} %get-tuple-element.50.lines, ...), custom_call_target="tpu_custom_call" | custom-call | tf_op jit(solution)/shard_map/place_receptors/pallas_call | solution.py:503
Async XLA Ops:
  2.6 23.6 %collective-permute-start.2 = (f32[6,4,128]{2,1,0:T(4,128)S(1)}, f32[6,4,128]{2,1,0:T(4,128)S(1)}, u32[]{:S(2)}, u32[]{:S(2)}) collective-permute-start(f32[6,4,128]{2,1,0:T(4,128)S(1)} %get-tuple-element.32), channel_id=1, source_target_pairs={{0,1},{1,2},{2,3},{3,4},{4,5},{5,6},{6,7},{7,8},{8,9},{9,10},{10,1... | collective-permute-start | bytes 36872 | tf_op jit(solution)/shard_map/ppermute | solution.py:387
  6.6 19.6 %collective-permute-start.3 = (f32[6,4,128]{2,1,0:T(4,128)S(1)}, f32[6,4,128]{2,1,0:T(4,128)S(1)}, u32[]{:S(2)}, u32[]{:S(2)}) collective-permute-start(f32[6,4,128]{2,1,0:T(4,128)S(1)} %get-tuple-element.33), channel_id=1, source_target_pairs={{1,0},{2,1},{3,2},{4,3},{5,4},{6,5},{7,6},{8,7},{9,8},{10,9},{11,1... | collective-permute-start | bytes 36872 | tf_op jit(solution)/shard_map/ppermute | solution.py:388
  15.4 10.8 %collective-permute-start = (f32[6,32,128]{2,1,0:T(8,128)S(1)}, f32[6,32,128]{2,1,0:T(8,128)S(1)}, u32[]{:S(2)}, u32[]{:S(2)}) collective-permute-start(f32[6,32,128]{2,1,0:T(8,128)S(1)} %get-tuple-element.30), channel_id=1, source_target_pairs={{0,32},{32,64},{64,96},{96,128},{128,160},{160,192},{192,224},{224... | collective-permute-start | bytes 294920 | tf_op jit(solution)/shard_map/ppermute | solution.py:387
  19.5 6.7 %collective-permute-start.1 = (f32[6,32,128]{2,1,0:T(8,128)S(1)}, f32[6,32,128]{2,1,0:T(8,128)S(1)}, u32[]{:S(2)}, u32[]{:S(2)}) collective-permute-start(f32[6,32,128]{2,1,0:T(8,128)S(1)} %get-tuple-element.31), channel_id=1, source_target_pairs={{32,0},{64,32},{96,64},{128,96},{160,128},{192,160},{224,192},{256... | collective-permute-start | bytes 294920 | tf_op jit(solution)/shard_map/ppermute | solution.py:388

commit v5 on v4

--- a/solution.py
+++ b/solution.py
@@ -16,6 +16,7 @@
 HALF = 32
 BY_MATRIX = 4
 STEPS = 1048000.0
+PARTS = 8
 
 
 def entry(number, f, g):
@@ -290,7 +291,7 @@
         words, scales, lambda f: jnp.concatenate([near[0, f], near[1, f]], axis=0)
     )
 
-    @pl.loop(0, blocks, unroll=8)
+    @pl.loop(0, blocks, unroll=16)
     def _(number):
         found = gather(table, words, scales, INNER, inner_cells, inner_shares, number)
         for f in range(FIELDS):
@@ -340,30 +341,37 @@
     fill_table(table, FIELDS * HALF, 1, jnp.zeros_like(edges))
     fill_words(words, scales, lambda f: rim[f])
 
-    @pl.loop(0, blocks, unroll=8)
+    @pl.loop(0, blocks, unroll=16)
     def _(number):
         found = gather(table, words, scales, RIM, rim_cells, shares, number)
         for f in range(FIELDS):
             values[number, f : f + 1, :] = found[f] + part[number, f : f + 1, :]
 
 
-def place_kernel(incoming, near, rim, lines, pick, taken, updated, high, low):
+def place_kernel(incoming, near, rim, lines, pick, taken, updated, *parts):
     blocks = incoming.shape[0]
     width_y = near.shape[2]
-    for number in range(blocks):
-        span = slice(number * LANES, (number + 1) * LANES)
-        value = incoming[number]
-        upper = value.astype(jnp.bfloat16).astype(jnp.float32)
-        lower = value - upper
-        for f in range(FIELDS):
-            for part, target in ((upper, high), (lower, low)):
-                wide = jnp.broadcast_to(part[f : f + 1], (16, LANES)).astype(jnp.bfloat16)
-                for first in range(0, INNER, 16):
-                    target[f * INNER + first : f * INNER + first + 16, span] = (
-                        lines[first : first + 16, span] * wide
-                    )
-    placed = jnp.dot(high[...], pick[...], preferred_element_type=jnp.float32)
-    placed = placed + jnp.dot(low[...], pick[...], preferred_element_type=jnp.float32)
+    each = blocks // len(parts)
+    placed = None
+    for first_block, part in zip(range(0, blocks, each), parts):
+        for number in range(first_block, first_block + each):
+            span = slice(number * LANES, (number + 1) * LANES)
+            column = (number - first_block) * LANES
+            value = incoming[number]
+            upper = value.astype(jnp.bfloat16).astype(jnp.float32)
+            lower = value - upper
+            for f in range(FIELDS):
+                for values, start in ((upper, column), (lower, column + each * LANES)):
+                    wide = jnp.broadcast_to(values[f : f + 1], (16, LANES)).astype(jnp.bfloat16)
+                    for first in range(0, INNER, 16):
+                        part[f * INNER + first : f * INNER + first + 16, start : start + LANES] = (
+                            lines[first : first + 16, span] * wide
+                        )
+        chosen = pick[first_block * LANES : (first_block + each) * LANES]
+        found = jnp.dot(
+            part[...], jnp.concatenate([chosen, chosen], axis=0), preferred_element_type=jnp.float32
+        )
+        placed = found if placed is None else placed + found
     for plane in range(4):
         rows = (plane % 2) * width_y
         lanes = slice((plane // 2) * LANES, (plane // 2 + 1) * LANES)
@@ -505,7 +513,7 @@
         out_shape=like(flow.shape, f32),
         in_specs=[vmem] * 6,
         out_specs=vmem,
-        scratch_shapes=[pltpu.VMEM((fields * INNER, blocks * LANES), jnp.bfloat16)] * 2,
+        scratch_shapes=[pltpu.VMEM((fields * INNER, 2 * blocks * LANES // PARTS), jnp.bfloat16)] * PARTS,
         compiler_params=params,
         name="place_receptors",
     )(incoming, near, rim, lines, pick, taken)

time: 49.1 us -> 48.6 us (0.990)
  Pallas kernels: 12.8 us -> 12.3 us
  transfers between devices with their start and end apart: 4 -> 4, of which waited for: 0 -> 0; matrix products, arithmetic and copies ran while one was open for 0% -> 0% of each run, Pallas kernels for 10% -> 9%
where the time goes in v5:
time: 48.6 us; the launch traced here: 48.3 us
  starting transfers between devices  18.8 us (39%)
  blocking collectives  16.5 us (34%)
  Pallas kernels  12.3 us (25%)
  between operations  0.72 us (1%)
    all_to_all x1, blocking collectives, shards(): lax.all_to_all(values, 'blk', split_axis=0, concat_axis=0, tiled=True)  16.5 us
    ppermute x2, starting transfers between devices, halo(): lax.ppermute(head, axis, [(i + 1, i) for i in range(ends)])  10.8 us
    ppermute x2, starting transfers between devices, halo(): lax.ppermute(tail, axis, [(i, i + 1) for i in range(ends)])  8.05 us
    pallas_call x1, Pallas kernels, shards(): pl.pallas_call(inner_kernel, out_shape=[like((blocks, fields, length), f3...  4.43 us
    pallas_call x1, Pallas kernels, shards(): pl.pallas_call(rim_kernel, out_shape=[like((blocks, fields, length), f32)...  4.18 us
    pallas_call x1, Pallas kernels, shards(): pl.pallas_call(load_kernel, out_shape=[like((fields, width_y, length), f3...  1.91 us
    pallas_call x1, Pallas kernels, shards(): pl.pallas_call(place_kernel, out_shape=like(flow.shape, f32), in_specs=[v...  1.75 us
  transfers between devices with their start and end apart: 4, of which 0 were waited for; matrix products, arithmetic and copies ran while one was open for 0% of the time, Pallas kernels for 9%

profile of v5, /device:TPU:7, one launch (start us, length us, event | category | flops | bytes accessed | tf_op | source)
XLA Modules:
  0.0 48.3 jit_solution(2967096498430841762)
XLA Ops:
  0.7 1.9 %load_block.1 = (f32[6,32,128]{2,1,0:T(8,128)S(1)}, f32[6,32,128]{2,1,0:T(8,128)S(1)}, f32[6,4,128]{2,1,0:T(4,128)S(1)}, f32[6,4,128]{2,1,0:T(4,128)S(1)}, f32[4...) custom-call(f32[6,4,6]{2,1,0:T(4,128)} %bitcast.13, ...), custom_call_target="tpu_custom_call" | custom-call | tf_op jit(solution)/shard_map/load_block/pallas_call | solution.py:435
  2.6 4.0 %collective-permute-start.2 = (f32[6,4,128]{2,1,0:T(4,128)S(1)}, f32[6,4,128]{2,1,0:T(4,128)S(1)}, u32[]{:S(2)}, u32[]{:S(2)}) collective-permute-start(f32[6,4,128]{2,1,0:T(4,128)S(1)} %get-tuple-element.32), channel_id=1, source_target_pairs={{0,1},{1,2},{2,3},{3,4},{4,5},{5,6},{6,7},{7,8},{8,9},{9,10},{10,1... | collective-permute-start | bytes 36872 | tf_op jit(solution)/shard_map/ppermute | solution.py:395
  6.6 8.9 %collective-permute-start.3 = (f32[6,4,128]{2,1,0:T(4,128)S(1)}, f32[6,4,128]{2,1,0:T(4,128)S(1)}, u32[]{:S(2)}, u32[]{:S(2)}) collective-permute-start(f32[6,4,128]{2,1,0:T(4,128)S(1)} %get-tuple-element.33), channel_id=1, source_target_pairs={{1,0},{2,1},{3,2},{4,3},{5,4},{6,5},{7,6},{8,7},{9,8},{10,9},{11,1... | collective-permute-start | bytes 36872 | tf_op jit(solution)/shard_map/ppermute | solution.py:396
  15.4 4.0 %collective-permute-start = (f32[6,32,128]{2,1,0:T(8,128)S(1)}, f32[6,32,128]{2,1,0:T(8,128)S(1)}, u32[]{:S(2)}, u32[]{:S(2)}) collective-permute-start(f32[6,32,128]{2,1,0:T(8,128)S(1)} %get-tuple-element.30), channel_id=1, source_target_pairs={{0,32},{32,64},{64,96},{96,128},{128,160},{160,192},{192,224},{224... | collective-permute-start | bytes 294920 | tf_op jit(solution)/shard_map/ppermute | solution.py:395
  19.5 1.9 %collective-permute-start.1 = (f32[6,32,128]{2,1,0:T(8,128)S(1)}, f32[6,32,128]{2,1,0:T(8,128)S(1)}, u32[]{:S(2)}, u32[]{:S(2)}) collective-permute-start(f32[6,32,128]{2,1,0:T(8,128)S(1)} %get-tuple-element.31), channel_id=1, source_target_pairs={{32,0},{64,32},{96,64},{128,96},{160,128},{192,160},{224,192},{256... | collective-permute-start | bytes 294920 | tf_op jit(solution)/shard_map/ppermute | solution.py:396
  21.4 4.4 %inner_lines.1 = (f32[16,6,128]{2,1,0:T(8,128)S(1)}, f32[2,6,32,128]{3,2,1,0:T(8,128)S(1)}, f32[6,72,128]{2,1,0:T(8,128)S(1)}, f32[72,128]{1,0:T(8,128)S(1)}, f3...) custom-call(f32[288,128]{1,0:T(8,128)S(1)} %get-tuple-element.29.matrice, ...), custom_call_target="tpu_custom_call" | custom-call | flops 10000000000 | bytes 3000000 | tf_op jit(solution)/shard_map/inner_lines/pallas_call | solution.py:464
  25.8 0.0 collective-permute-done.2.y_prev
  25.9 0.0 collective-permute-done.3.y_next
  25.9 0.0 collective-permute-done.x_prev
  25.9 0.0 collective-permute-done.1.x_next
  25.9 4.2 %rim_lines.1 = (f32[16,6,128]{2,1,0:T(8,128)S(1)}, f32[6,72,128]{2,1,0:T(8,128)S(1)}) custom-call(f32[288,128]{1,0:T(8,128)S(1)} %get-tuple-element.29.matrices, f32[6,32,128]{2,1,0:T(8,128)S(1)} %collective-permute-done.x_prev, f32[6,32,128]{2,1,0:T(8,128)S(1)} %collective-permute-done.1.x_next, f32[6,4,128]{2,1,0:T(4,128)S(1)} %collective-permute-done.2.y_prev, ...), custom_call_target="tpu_custom_call" | custom-call | tf_op jit(solution)/shard_map/rim_lines/pallas_call | solution.py:493
  30.1 16.5 %all_to_all.5.incoming = f32[16,6,128]{2,1,0:T(8,128)S(1)} all-to-all(f32[16,6,128]{2,1,0:T(8,128)S(1)} %get-tuple-element.47), channel_id=1, replica_groups=mesh['blk'=16,'bal'=32] {'blk'}, dimensions={0} | all-to-all | bytes 98304 | tf_op jit(solution)/shard_map/all_to_all | solution.py:510
  46.5 1.8 %place_receptors.1 = f32[4,6,32,128]{3,2,1,0:T(8,128)} custom-call(f32[16,6,128]{2,1,0:T(8,128)S(1)} %all_to_all.5.incoming, f32[2,6,32,128]{3,2,1,0:T(8,128)S(1)} %get-tuple-element.48.near, f32[6,72,128]{2,1,0:T(8,128)S(1)} %get-tuple-element.49.rim, bf16[64,2048]{1,0:T(8,128)(2,1)S(1)} %get-tuple-element.50.lines, ...), custom_call_target="tpu_custom_call" | custom-call | tf_op jit(solution)/shard_map/place_receptors/pallas_call | solution.py:511
Async XLA Ops:
  2.6 23.3 %collective-permute-start.2 = (f32[6,4,128]{2,1,0:T(4,128)S(1)}, f32[6,4,128]{2,1,0:T(4,128)S(1)}, u32[]{:S(2)}, u32[]{:S(2)}) collective-permute-start(f32[6,4,128]{2,1,0:T(4,128)S(1)} %get-tuple-element.32), channel_id=1, source_target_pairs={{0,1},{1,2},{2,3},{3,4},{4,5},{5,6},{6,7},{7,8},{8,9},{9,10},{10,1... | collective-permute-start | bytes 36872 | tf_op jit(solution)/shard_map/ppermute | solution.py:395
  6.6 19.3 %collective-permute-start.3 = (f32[6,4,128]{2,1,0:T(4,128)S(1)}, f32[6,4,128]{2,1,0:T(4,128)S(1)}, u32[]{:S(2)}, u32[]{:S(2)}) collective-permute-start(f32[6,4,128]{2,1,0:T(4,128)S(1)} %get-tuple-element.33), channel_id=1, source_target_pairs={{1,0},{2,1},{3,2},{4,3},{5,4},{6,5},{7,6},{8,7},{9,8},{10,9},{11,1... | collective-permute-start | bytes 36872 | tf_op jit(solution)/shard_map/ppermute | solution.py:396
  15.4 10.4 %collective-permute-start = (f32[6,32,128]{2,1,0:T(8,128)S(1)}, f32[6,32,128]{2,1,0:T(8,128)S(1)}, u32[]{:S(2)}, u32[]{:S(2)}) collective-permute-start(f32[6,32,128]{2,1,0:T(8,128)S(1)} %get-tuple-element.30), channel_id=1, source_target_pairs={{0,32},{32,64},{64,96},{96,128},{128,160},{160,192},{192,224},{224... | collective-permute-start | bytes 294920 | tf_op jit(solution)/shard_map/ppermute | solution.py:395
  19.5 6.4 %collective-permute-start.1 = (f32[6,32,128]{2,1,0:T(8,128)S(1)}, f32[6,32,128]{2,1,0:T(8,128)S(1)}, u32[]{:S(2)}, u32[]{:S(2)}) collective-permute-start(f32[6,32,128]{2,1,0:T(8,128)S(1)} %get-tuple-element.31), channel_id=1, source_target_pairs={{32,0},{64,32},{96,64},{128,96},{160,128},{192,160},{224,192},{256... | collective-permute-start | bytes 294920 | tf_op jit(solution)/shard_map/ppermute | solution.py:396

commit v6 on v5

--- a/solution.py
+++ b/solution.py
@@ -159,7 +159,7 @@
 def load_kernel(
     jac_in, coupling_in, inverse_in, units_in, order_in, receptor_in,
     flow_in, source_in, diag_in, cells_in, weights_in,
-    x_head, x_tail, y_head, y_tail, flow, source, diag, cells, weights,
+    x_even, x_odd, y_even, y_odd, flow, source, diag, cells, weights,
     live, lines, pick, taken, matrices,
     jac, coupling, inverse, units, order, receptor, done,
 ):
@@ -175,8 +175,6 @@
                 (order_in, order),
                 (receptor_in, receptor),
                 (flow_in, flow),
-                (flow_in.at[0], x_head),
-                (flow_in.at[width_x - 1], x_tail),
                 (source_in, source),
                 (diag_in, diag),
                 (cells_in, cells),
@@ -208,10 +206,15 @@
     )
     prepare(receptor, lines, pick, taken)
     copies[6].wait()
+    upward = lax.rem(lax.axis_index("blk"), 2) == 0
+    x_even[...] = jnp.where(upward, flow[width_x - 1], flow[0])
+    x_odd[...] = jnp.where(upward, flow[0], flow[width_x - 1])
+    upward = lax.rem(lax.axis_index("bal"), 2) == 0
     for f in range(FIELDS):
         for x in range(width_x):
-            y_head[f, x : x + 1] = flow[x, f, 0:1]
-            y_tail[f, x : x + 1] = flow[x, f, width_y - 1 : width_y]
+            head, tail = flow[x, f, 0:1], flow[x, f, width_y - 1 : width_y]
+            y_even[f, x : x + 1] = jnp.where(upward, tail, head)
+            y_odd[f, x : x + 1] = jnp.where(upward, head, tail)
     for copy in copies[7:]:
         copy.wait()
 
@@ -299,19 +302,23 @@
 
 
 def rim_kernel(
-    matrices, x_prev, x_next, y_prev, y_next,
+    matrices, x_even, x_odd, y_even, y_odd,
     part, rim_residual, rim_scale, rim_live, rim_flow, rim_cells, shares,
     values, rim, residual, table, words, scales,
 ):
-    width_y = x_prev.shape[1]
+    width_y = x_even.shape[1]
+    x_upward = lax.rem(lax.axis_index("blk"), 2) == 0
+    y_upward = lax.rem(lax.axis_index("bal"), 2) == 0
     blocks = rim_cells.shape[1]
-    for number, (side, halo) in enumerate(((0, x_prev), (1, x_next))):
+    for number, (side, halo) in enumerate(((0, (x_odd, x_even)), (1, (x_even, x_odd)))):
         rows = slice(number * width_y, (number + 1) * width_y)
-        added = apply(lambda f, g: matrices[entry(4 + side, f, g)], [halo[g] for g in range(FIELDS)])
+        lines = [jnp.where(x_upward, halo[0][g], halo[1][g]) for g in range(FIELDS)]
+        added = apply(lambda f, g: matrices[entry(4 + side, f, g)], lines)
         for f in range(FIELDS):
             residual[f, rows] = rim_residual[f, rows] + added[f]
-    for number, (side, halo) in enumerate(((2, y_prev), (3, y_next))):
-        added = apply(lambda f, g: matrices[entry(4 + side, f, g)], [halo[g] for g in range(FIELDS)])
+    for number, (side, halo) in enumerate(((2, (y_odd, y_even)), (3, (y_even, y_odd)))):
+        lines = [jnp.where(y_upward, halo[0][g], halo[1][g]) for g in range(FIELDS)]
+        added = apply(lambda f, g: matrices[entry(4 + side, f, g)], lines)
         for f in range(FIELDS):
             at_row = 64 + 2 * number
             residual[f, at_row : at_row + 2] = (
@@ -390,11 +397,13 @@
                 )
 
 
-def halo(ends, axis, head, tail):
-    return (
-        lax.ppermute(tail, axis, [(i, i + 1) for i in range(ends)]),
-        lax.ppermute(head, axis, [(i + 1, i) for i in range(ends)]),
-    )
+def swap(axis, even, odd):
+    count = lax.axis_size(axis)
+    out = []
+    for first, lines in ((0, even), (1, odd)):
+        pairs = [(i, i + 1) for i in range(first, count - 1, 2)]
+        out.append(lax.ppermute(lines, axis, pairs + [(j, i) for i, j in pairs]))
+    return out
 
 
 def shards(
@@ -453,14 +462,12 @@
             pltpu.SMEM(active_units.shape, i32),
             pltpu.VMEM((1, LANES), i32),
             pltpu.VMEM(receptor.shape, i32),
-            pltpu.SemaphoreType.DMA((13,)),
+            pltpu.SemaphoreType.DMA((11,)),
         ],
         compiler_params=params,
         name="load_block",
     )(*raw)
-    x_head, x_tail, y_head, y_tail = edges
-    x_prev, x_next = halo(lax.axis_size("blk") - 1, "blk", x_head, x_tail)
-    y_prev, y_next = halo(lax.axis_size("bal") - 1, "bal", y_head, y_tail)
+    halos = swap("blk", *edges[:2]) + swap("bal", *edges[2:])
     part, near, *rest = pl.pallas_call(
         inner_kernel,
         out_shape=[
@@ -506,7 +513,7 @@
         ],
         compiler_params=params,
         name="rim_lines",
-    )(matrices, x_prev, x_next, y_prev, y_next, part, *rest)
+    )(matrices, *halos, part, *rest)
     incoming = lax.all_to_all(values, "blk", split_axis=0, concat_axis=0, tiled=True)
     updated = pl.pallas_call(
         place_kernel,

time: 48.6 us -> 47 us (0.967)
  blocking collectives: 16.5 us -> 14.3 us
  starting transfers between devices: 18.8 us -> 19.4 us
    all_to_all x1, blocking collectives: 16.5 us -> 14.3 us  [shards(): lax.all_to_all(values, 'blk', split_axis=0, concat_axis=0, tiled=True)]
    ppermute x4, starting transfers between devices: 18.8 us -> 19.4 us  [swap(): out.append(lax.ppermute(lines, axis, pairs + [(j, i) for i, j in pairs]))]
where the time goes in v6:
time: 47 us; the launch traced here: 46.7 us
  starting transfers between devices  19.4 us (41%)
  blocking collectives  14.3 us (30%)
  Pallas kernels  12.3 us (26%)
  between operations  0.72 us (2%)
    ppermute x4, starting transfers between devices, swap(): out.append(lax.ppermute(lines, axis, pairs + [(j, i) for i, j in pairs]))  19.4 us
    all_to_all x1, blocking collectives, shards(): lax.all_to_all(values, 'blk', split_axis=0, concat_axis=0, tiled=True)  14.3 us
    pallas_call x1, Pallas kernels, shards(): pl.pallas_call(inner_kernel, out_shape=[like((blocks, fields, length), f3...  4.43 us
    pallas_call x1, Pallas kernels, shards(): pl.pallas_call(rim_kernel, out_shape=[like((blocks, fields, length), f32)...  4.19 us
    pallas_call x1, Pallas kernels, shards(): pl.pallas_call(load_kernel, out_shape=[like((fields, width_y, length), f3...  1.9 us
    pallas_call x1, Pallas kernels, shards(): pl.pallas_call(place_kernel, out_shape=like(flow.shape, f32), in_specs=[v...  1.75 us
  transfers between devices with their start and end apart: 4, of which 0 were waited for; matrix products, arithmetic and copies ran while one was open for 0% of the time, Pallas kernels for 9%

profile of v6, /device:TPU:7, one launch (start us, length us, event | category | flops | bytes accessed | tf_op | source)
XLA Modules:
  0.0 46.7 jit_solution(10845623917349060288)
XLA Ops:
  0.7 1.9 %load_block.1 = (f32[6,32,128]{2,1,0:T(8,128)S(1)}, f32[6,32,128]{2,1,0:T(8,128)S(1)}, f32[6,4,128]{2,1,0:T(4,128)S(1)}, f32[6,4,128]{2,1,0:T(4,128)S(1)}, f32[4...) custom-call(f32[6,4,6]{2,1,0:T(4,128)} %bitcast.13, ...), custom_call_target="tpu_custom_call" | custom-call | tf_op jit(solution)/shard_map/load_block/pallas_call | solution.py:444
  2.6 4.0 %collective-permute-start.2 = (f32[6,4,128]{2,1,0:T(4,128)S(1)}, f32[6,4,128]{2,1,0:T(4,128)S(1)}, u32[]{:S(2)}, u32[]{:S(2)}) collective-permute-start(f32[6,4,128]{2,1,0:T(4,128)S(1)} %get-tuple-element.32), channel_id=1, source_target_pairs={{0,1},{2,3},{4,5},{6,7},{8,9},{10,11},{12,13},{14,15},{16,17},{18,... | collective-permute-start | bytes 36872 | tf_op jit(solution)/shard_map/ppermute | solution.py:405
  6.6 9.1 %collective-permute-start.3 = (f32[6,4,128]{2,1,0:T(4,128)S(1)}, f32[6,4,128]{2,1,0:T(4,128)S(1)}, u32[]{:S(2)}, u32[]{:S(2)}) collective-permute-start(f32[6,4,128]{2,1,0:T(4,128)S(1)} %get-tuple-element.33), channel_id=1, source_target_pairs={{1,2},{3,4},{5,6},{7,8},{9,10},{11,12},{13,14},{15,16},{17,18},{19... | collective-permute-start | bytes 36872 | tf_op jit(solution)/shard_map/ppermute | solution.py:405
  15.7 3.1 %collective-permute-start = (f32[6,32,128]{2,1,0:T(8,128)S(1)}, f32[6,32,128]{2,1,0:T(8,128)S(1)}, u32[]{:S(2)}, u32[]{:S(2)}) collective-permute-start(f32[6,32,128]{2,1,0:T(8,128)S(1)} %get-tuple-element.30), channel_id=1, source_target_pairs={{0,32},{64,96},{128,160},{192,224},{256,288},{320,352},{384,416},{... | collective-permute-start | bytes 294920 | tf_op jit(solution)/shard_map/ppermute | solution.py:405
  18.8 3.1 %collective-permute-start.1 = (f32[6,32,128]{2,1,0:T(8,128)S(1)}, f32[6,32,128]{2,1,0:T(8,128)S(1)}, u32[]{:S(2)}, u32[]{:S(2)}) collective-permute-start(f32[6,32,128]{2,1,0:T(8,128)S(1)} %get-tuple-element.31), channel_id=1, source_target_pairs={{32,64},{96,128},{160,192},{224,256},{288,320},{352,384},{416,448}... | collective-permute-start | bytes 294920 | tf_op jit(solution)/shard_map/ppermute | solution.py:405
  22.0 4.4 %inner_lines.1 = (f32[16,6,128]{2,1,0:T(8,128)S(1)}, f32[2,6,32,128]{3,2,1,0:T(8,128)S(1)}, f32[6,72,128]{2,1,0:T(8,128)S(1)}, f32[72,128]{1,0:T(8,128)S(1)}, f3...) custom-call(f32[288,128]{1,0:T(8,128)S(1)} %get-tuple-element.29.matrice, ...), custom_call_target="tpu_custom_call" | custom-call | flops 10000000000 | bytes 3000000 | tf_op jit(solution)/shard_map/inner_lines/pallas_call | solution.py:471
  26.4 0.0 collective-permute-done.2.y_even
  26.4 0.0 collective-permute-done.3.y_odd
  26.4 0.0 collective-permute-done.x_even
  26.4 0.0 collective-permute-done.1.x_odd
  26.4 4.2 %rim_lines.1 = (f32[16,6,128]{2,1,0:T(8,128)S(1)}, f32[6,72,128]{2,1,0:T(8,128)S(1)}) custom-call(f32[288,128]{1,0:T(8,128)S(1)} %get-tuple-element.29.matrices, f32[6,32,128]{2,1,0:T(8,128)S(1)} %collective-permute-done.x_even, f32[6,32,128]{2,1,0:T(8,128)S(1)} %collective-permute-done.1.x_odd, f32[6,4,128]{2,1,0:T(4,128)S(1)} %collective-permute-done.2.y_even, ...), custom_call_target="tpu_custom_call" | custom-call | tf_op jit(solution)/shard_map/rim_lines/pallas_call | solution.py:500
  30.6 14.3 %all_to_all.5.incoming = f32[16,6,128]{2,1,0:T(8,128)S(1)} all-to-all(f32[16,6,128]{2,1,0:T(8,128)S(1)} %get-tuple-element.47), channel_id=1, replica_groups=mesh['blk'=16,'bal'=32] {'blk'}, dimensions={0} | all-to-all | bytes 98304 | tf_op jit(solution)/shard_map/all_to_all | solution.py:517
  44.9 1.8 %place_receptors.1 = f32[4,6,32,128]{3,2,1,0:T(8,128)} custom-call(f32[16,6,128]{2,1,0:T(8,128)S(1)} %all_to_all.5.incoming, f32[2,6,32,128]{3,2,1,0:T(8,128)S(1)} %get-tuple-element.48.near, f32[6,72,128]{2,1,0:T(8,128)S(1)} %get-tuple-element.49.rim, bf16[64,2048]{1,0:T(8,128)(2,1)S(1)} %get-tuple-element.50.lines, ...), custom_call_target="tpu_custom_call" | custom-call | tf_op jit(solution)/shard_map/place_receptors/pallas_call | solution.py:518
Async XLA Ops:
  2.6 23.8 %collective-permute-start.2 = (f32[6,4,128]{2,1,0:T(4,128)S(1)}, f32[6,4,128]{2,1,0:T(4,128)S(1)}, u32[]{:S(2)}, u32[]{:S(2)}) collective-permute-start(f32[6,4,128]{2,1,0:T(4,128)S(1)} %get-tuple-element.32), channel_id=1, source_target_pairs={{0,1},{2,3},{4,5},{6,7},{8,9},{10,11},{12,13},{14,15},{16,17},{18,... | collective-permute-start | bytes 36872 | tf_op jit(solution)/shard_map/ppermute | solution.py:405
  6.6 19.8 %collective-permute-start.3 = (f32[6,4,128]{2,1,0:T(4,128)S(1)}, f32[6,4,128]{2,1,0:T(4,128)S(1)}, u32[]{:S(2)}, u32[]{:S(2)}) collective-permute-start(f32[6,4,128]{2,1,0:T(4,128)S(1)} %get-tuple-element.33), channel_id=1, source_target_pairs={{1,2},{3,4},{5,6},{7,8},{9,10},{11,12},{13,14},{15,16},{17,18},{19... | collective-permute-start | bytes 36872 | tf_op jit(solution)/shard_map/ppermute | solution.py:405
  15.7 10.7 %collective-permute-start = (f32[6,32,128]{2,1,0:T(8,128)S(1)}, f32[6,32,128]{2,1,0:T(8,128)S(1)}, u32[]{:S(2)}, u32[]{:S(2)}) collective-permute-start(f32[6,32,128]{2,1,0:T(8,128)S(1)} %get-tuple-element.30), channel_id=1, source_target_pairs={{0,32},{64,96},{128,160},{192,224},{256,288},{320,352},{384,416},{... | collective-permute-start | bytes 294920 | tf_op jit(solution)/shard_map/ppermute | solution.py:405
  18.8 7.6 %collective-permute-start.1 = (f32[6,32,128]{2,1,0:T(8,128)S(1)}, f32[6,32,128]{2,1,0:T(8,128)S(1)}, u32[]{:S(2)}, u32[]{:S(2)}) collective-permute-start(f32[6,32,128]{2,1,0:T(8,128)S(1)} %get-tuple-element.31), channel_id=1, source_target_pairs={{32,64},{96,128},{160,192},{224,256},{288,320},{352,384},{416,448}... | collective-permute-start | bytes 294920 | tf_op jit(solution)/shard_map/ppermute | solution.py:405

commit v7 on v6

--- a/solution.py
+++ b/solution.py
@@ -302,7 +302,7 @@
 
 
 def rim_kernel(
-    matrices, x_even, x_odd, y_even, y_odd,
+    matrices, x_even, x_odd, y_odd, y_even,
     part, rim_residual, rim_scale, rim_live, rim_flow, rim_cells, shares,
     values, rim, residual, table, words, scales,
 ):
@@ -467,7 +467,7 @@
         compiler_params=params,
         name="load_block",
     )(*raw)
-    halos = swap("blk", *edges[:2]) + swap("bal", *edges[2:])
+    halos = swap("blk", *edges[:2]) + swap("bal", *edges[2:])[::-1]
     part, near, *rest = pl.pallas_call(
         inner_kernel,
         out_shape=[

time: 47 us -> 46.4 us (0.987)
  starting transfers between devices: 19.4 us -> 18.8 us
    ppermute x4, starting transfers between devices: 19.4 us -> 18.8 us  [swap(): out.append(lax.ppermute(lines, axis, pairs + [(j, i) for i, j in pairs]))]
  transfers between devices with their start and end apart: 4 -> 4, of which waited for: 0 -> 0; matrix products, arithmetic and copies ran while one was open for 0% -> 0% of each run, Pallas kernels for 9% -> 10%
where the time goes in v7:
time: 46.4 us; the launch traced here: 46.1 us
  starting transfers between devices  18.8 us (41%)
  blocking collectives  14.3 us (31%)
  Pallas kernels  12.3 us (27%)
  between operations  0.72 us (2%)
    ppermute x4, starting transfers between devices, swap(): out.append(lax.ppermute(lines, axis, pairs + [(j, i) for i, j in pairs]))  18.8 us
    all_to_all x1, blocking collectives, shards(): lax.all_to_all(values, 'blk', split_axis=0, concat_axis=0, tiled=True)  14.3 us
    pallas_call x1, Pallas kernels, shards(): pl.pallas_call(inner_kernel, out_shape=[like((blocks, fields, length), f3...  4.43 us
    pallas_call x1, Pallas kernels, shards(): pl.pallas_call(rim_kernel, out_shape=[like((blocks, fields, length), f32)...  4.19 us
    pallas_call x1, Pallas kernels, shards(): pl.pallas_call(load_kernel, out_shape=[like((fields, width_y, length), f3...  1.9 us
    pallas_call x1, Pallas kernels, shards(): pl.pallas_call(place_kernel, out_shape=like(flow.shape, f32), in_specs=[v...  1.75 us
  transfers between devices with their start and end apart: 4, of which 0 were waited for; matrix products, arithmetic and copies ran while one was open for 0% of the time, Pallas kernels for 10%

profile of v7, /device:TPU:7, one launch (start us, length us, event | category | flops | bytes accessed | tf_op | source)
XLA Modules:
  0.0 46.1 jit_solution(17235200202085755590)
XLA Ops:
  0.7 1.9 %load_block.1 = (f32[6,32,128]{2,1,0:T(8,128)S(1)}, f32[6,32,128]{2,1,0:T(8,128)S(1)}, f32[6,4,128]{2,1,0:T(4,128)S(1)}, f32[6,4,128]{2,1,0:T(4,128)S(1)}, f32[4...) custom-call(f32[6,4,6]{2,1,0:T(4,128)} %bitcast.13, ...), custom_call_target="tpu_custom_call" | custom-call | tf_op jit(solution)/shard_map/load_block/pallas_call | solution.py:444
  2.6 10.9 %collective-permute-start.2 = (f32[6,4,128]{2,1,0:T(4,128)S(1)}, f32[6,4,128]{2,1,0:T(4,128)S(1)}, u32[]{:S(2)}, u32[]{:S(2)}) collective-permute-start(f32[6,4,128]{2,1,0:T(4,128)S(1)} %get-tuple-element.32), channel_id=1, source_target_pairs={{1,2},{3,4},{5,6},{7,8},{9,10},{11,12},{13,14},{15,16},{17,18},{19... | collective-permute-start | bytes 36872 | tf_op jit(solution)/shard_map/ppermute | solution.py:405
  13.5 1.9 %collective-permute-start.3 = (f32[6,4,128]{2,1,0:T(4,128)S(1)}, f32[6,4,128]{2,1,0:T(4,128)S(1)}, u32[]{:S(2)}, u32[]{:S(2)}) collective-permute-start(f32[6,4,128]{2,1,0:T(4,128)S(1)} %get-tuple-element.33), channel_id=1, source_target_pairs={{0,1},{2,3},{4,5},{6,7},{8,9},{10,11},{12,13},{14,15},{16,17},{18,... | collective-permute-start | bytes 36872 | tf_op jit(solution)/shard_map/ppermute | solution.py:405
  15.4 2.9 %collective-permute-start = (f32[6,32,128]{2,1,0:T(8,128)S(1)}, f32[6,32,128]{2,1,0:T(8,128)S(1)}, u32[]{:S(2)}, u32[]{:S(2)}) collective-permute-start(f32[6,32,128]{2,1,0:T(8,128)S(1)} %get-tuple-element.30), channel_id=1, source_target_pairs={{0,32},{64,96},{128,160},{192,224},{256,288},{320,352},{384,416},{... | collective-permute-start | bytes 294920 | tf_op jit(solution)/shard_map/ppermute | solution.py:405
  18.3 3.1 %collective-permute-start.1 = (f32[6,32,128]{2,1,0:T(8,128)S(1)}, f32[6,32,128]{2,1,0:T(8,128)S(1)}, u32[]{:S(2)}, u32[]{:S(2)}) collective-permute-start(f32[6,32,128]{2,1,0:T(8,128)S(1)} %get-tuple-element.31), channel_id=1, source_target_pairs={{32,64},{96,128},{160,192},{224,256},{288,320},{352,384},{416,448}... | collective-permute-start | bytes 294920 | tf_op jit(solution)/shard_map/ppermute | solution.py:405
  21.4 4.4 %inner_lines.1 = (f32[16,6,128]{2,1,0:T(8,128)S(1)}, f32[2,6,32,128]{3,2,1,0:T(8,128)S(1)}, f32[6,72,128]{2,1,0:T(8,128)S(1)}, f32[72,128]{1,0:T(8,128)S(1)}, f3...) custom-call(f32[288,128]{1,0:T(8,128)S(1)} %get-tuple-element.29.matrice, ...), custom_call_target="tpu_custom_call" | custom-call | flops 10000000000 | bytes 3000000 | tf_op jit(solution)/shard_map/inner_lines/pallas_call | solution.py:471
  25.8 0.0 collective-permute-done.2.y_odd
  25.9 0.0 collective-permute-done.3.y_even
  25.9 0.0 collective-permute-done.x_even
  25.9 0.0 collective-permute-done.1.x_odd
  25.9 4.2 %rim_lines.1 = (f32[16,6,128]{2,1,0:T(8,128)S(1)}, f32[6,72,128]{2,1,0:T(8,128)S(1)}) custom-call(f32[288,128]{1,0:T(8,128)S(1)} %get-tuple-element.29.matrices, f32[6,32,128]{2,1,0:T(8,128)S(1)} %collective-permute-done.x_even, f32[6,32,128]{2,1,0:T(8,128)S(1)} %collective-permute-done.1.x_odd, f32[6,4,128]{2,1,0:T(4,128)S(1)} %collective-permute-done.2.y_odd, ...), custom_call_target="tpu_custom_call" | custom-call | tf_op jit(solution)/shard_map/rim_lines/pallas_call | solution.py:500
  30.1 14.3 %all_to_all.5.incoming = f32[16,6,128]{2,1,0:T(8,128)S(1)} all-to-all(f32[16,6,128]{2,1,0:T(8,128)S(1)} %get-tuple-element.47), channel_id=1, replica_groups=mesh['blk'=16,'bal'=32] {'blk'}, dimensions={0} | all-to-all | bytes 98304 | tf_op jit(solution)/shard_map/all_to_all | solution.py:517
  44.4 1.8 %place_receptors.1 = f32[4,6,32,128]{3,2,1,0:T(8,128)} custom-call(f32[16,6,128]{2,1,0:T(8,128)S(1)} %all_to_all.5.incoming, f32[2,6,32,128]{3,2,1,0:T(8,128)S(1)} %get-tuple-element.48.near, f32[6,72,128]{2,1,0:T(8,128)S(1)} %get-tuple-element.49.rim, bf16[64,2048]{1,0:T(8,128)(2,1)S(1)} %get-tuple-element.50.lines, ...), custom_call_target="tpu_custom_call" | custom-call | tf_op jit(solution)/shard_map/place_receptors/pallas_call | solution.py:518
Async XLA Ops:
  2.6 23.3 %collective-permute-start.2 = (f32[6,4,128]{2,1,0:T(4,128)S(1)}, f32[6,4,128]{2,1,0:T(4,128)S(1)}, u32[]{:S(2)}, u32[]{:S(2)}) collective-permute-start(f32[6,4,128]{2,1,0:T(4,128)S(1)} %get-tuple-element.32), channel_id=1, source_target_pairs={{1,2},{3,4},{5,6},{7,8},{9,10},{11,12},{13,14},{15,16},{17,18},{19... | collective-permute-start | bytes 36872 | tf_op jit(solution)/shard_map/ppermute | solution.py:405
  13.5 12.4 %collective-permute-start.3 = (f32[6,4,128]{2,1,0:T(4,128)S(1)}, f32[6,4,128]{2,1,0:T(4,128)S(1)}, u32[]{:S(2)}, u32[]{:S(2)}) collective-permute-start(f32[6,4,128]{2,1,0:T(4,128)S(1)} %get-tuple-element.33), channel_id=1, source_target_pairs={{0,1},{2,3},{4,5},{6,7},{8,9},{10,11},{12,13},{14,15},{16,17},{18,... | collective-permute-start | bytes 36872 | tf_op jit(solution)/shard_map/ppermute | solution.py:405
  15.4 10.4 %collective-permute-start = (f32[6,32,128]{2,1,0:T(8,128)S(1)}, f32[6,32,128]{2,1,0:T(8,128)S(1)}, u32[]{:S(2)}, u32[]{:S(2)}) collective-permute-start(f32[6,32,128]{2,1,0:T(8,128)S(1)} %get-tuple-element.30), channel_id=1, source_target_pairs={{0,32},{64,96},{128,160},{192,224},{256,288},{320,352},{384,416},{... | collective-permute-start | bytes 294920 | tf_op jit(solution)/shard_map/ppermute | solution.py:405
  18.3 7.6 %collective-permute-start.1 = (f32[6,32,128]{2,1,0:T(8,128)S(1)}, f32[6,32,128]{2,1,0:T(8,128)S(1)}, u32[]{:S(2)}, u32[]{:S(2)}) collective-permute-start(f32[6,32,128]{2,1,0:T(8,128)S(1)} %get-tuple-element.31), channel_id=1, source_target_pairs={{32,64},{96,128},{160,192},{224,256},{288,320},{352,384},{416,448}... | collective-permute-start | bytes 294920 | tf_op jit(solution)/shard_map/ppermute | solution.py:405

commit v8 on v7

--- a/solution.py
+++ b/solution.py
@@ -302,7 +302,7 @@
 
 
 def rim_kernel(
-    matrices, x_even, x_odd, y_odd, y_even,
+    matrices, x_odd, x_even, y_odd, y_even,
     part, rim_residual, rim_scale, rim_live, rim_flow, rim_cells, shares,
     values, rim, residual, table, words, scales,
 ):
@@ -467,7 +467,7 @@
         compiler_params=params,
         name="load_block",
     )(*raw)
-    halos = swap("blk", *edges[:2]) + swap("bal", *edges[2:])[::-1]
+    halos = swap("blk", *edges[:2])[::-1] + swap("bal", *edges[2:])[::-1]
     part, near, *rest = pl.pallas_call(
         inner_kernel,
         out_shape=[

time: 46.4 us -> 46.5 us (level)
  no operation moved by 1% of the time
where the time goes in v8:
time: 46.5 us; the launch traced here: 46.1 us
  starting transfers between devices  18.8 us (40%)
  blocking collectives  14.3 us (31%)
  Pallas kernels  12.3 us (26%)
  between operations  0.72 us (2%)
    ppermute x4, starting transfers between devices, swap(): out.append(lax.ppermute(lines, axis, pairs + [(j, i) for i, j in pairs]))  18.8 us
    all_to_all x1, blocking collectives, shards(): lax.all_to_all(values, 'blk', split_axis=0, concat_axis=0, tiled=True)  14.3 us
    pallas_call x1, Pallas kernels, shards(): pl.pallas_call(inner_kernel, out_shape=[like((blocks, fields, length), f3...  4.43 us
    pallas_call x1, Pallas kernels, shards(): pl.pallas_call(rim_kernel, out_shape=[like((blocks, fields, length), f32)...  4.19 us
    pallas_call x1, Pallas kernels, shards(): pl.pallas_call(load_kernel, out_shape=[like((fields, width_y, length), f3...  1.9 us
    pallas_call x1, Pallas kernels, shards(): pl.pallas_call(place_kernel, out_shape=like(flow.shape, f32), in_specs=[v...  1.75 us
  transfers between devices with their start and end apart: 4, of which 0 were waited for; matrix products, arithmetic and copies ran while one was open for 0% of the time, Pallas kernels for 10%

profile of v8, /device:TPU:7, one launch (start us, length us, event | category | flops | bytes accessed | tf_op | source)
XLA Modules:
  0.0 46.1 jit_solution(5165859691330297835)
XLA Ops:
  0.7 1.9 %load_block.1 = (f32[6,32,128]{2,1,0:T(8,128)S(1)}, f32[6,32,128]{2,1,0:T(8,128)S(1)}, f32[6,4,128]{2,1,0:T(4,128)S(1)}, f32[6,4,128]{2,1,0:T(4,128)S(1)}, f32[4...) custom-call(f32[6,4,6]{2,1,0:T(4,128)} %bitcast.13, ...), custom_call_target="tpu_custom_call" | custom-call | tf_op jit(solution)/shard_map/load_block/pallas_call | solution.py:444
  2.6 10.9 %collective-permute-start.2 = (f32[6,4,128]{2,1,0:T(4,128)S(1)}, f32[6,4,128]{2,1,0:T(4,128)S(1)}, u32[]{:S(2)}, u32[]{:S(2)}) collective-permute-start(f32[6,4,128]{2,1,0:T(4,128)S(1)} %get-tuple-element.32), channel_id=1, source_target_pairs={{1,2},{3,4},{5,6},{7,8},{9,10},{11,12},{13,14},{15,16},{17,18},{19... | collective-permute-start | bytes 36872 | tf_op jit(solution)/shard_map/ppermute | solution.py:405
  13.5 1.9 %collective-permute-start.3 = (f32[6,4,128]{2,1,0:T(4,128)S(1)}, f32[6,4,128]{2,1,0:T(4,128)S(1)}, u32[]{:S(2)}, u32[]{:S(2)}) collective-permute-start(f32[6,4,128]{2,1,0:T(4,128)S(1)} %get-tuple-element.33), channel_id=1, source_target_pairs={{0,1},{2,3},{4,5},{6,7},{8,9},{10,11},{12,13},{14,15},{16,17},{18,... | collective-permute-start | bytes 36872 | tf_op jit(solution)/shard_map/ppermute | solution.py:405
  15.4 4.0 %collective-permute-start = (f32[6,32,128]{2,1,0:T(8,128)S(1)}, f32[6,32,128]{2,1,0:T(8,128)S(1)}, u32[]{:S(2)}, u32[]{:S(2)}) collective-permute-start(f32[6,32,128]{2,1,0:T(8,128)S(1)} %get-tuple-element.30), channel_id=1, source_target_pairs={{32,64},{96,128},{160,192},{224,256},{288,320},{352,384},{416,448}... | collective-permute-start | bytes 294920 | tf_op jit(solution)/shard_map/ppermute | solution.py:405
  19.5 1.9 %collective-permute-start.1 = (f32[6,32,128]{2,1,0:T(8,128)S(1)}, f32[6,32,128]{2,1,0:T(8,128)S(1)}, u32[]{:S(2)}, u32[]{:S(2)}) collective-permute-start(f32[6,32,128]{2,1,0:T(8,128)S(1)} %get-tuple-element.31), channel_id=1, source_target_pairs={{0,32},{64,96},{128,160},{192,224},{256,288},{320,352},{384,416},{... | collective-permute-start | bytes 294920 | tf_op jit(solution)/shard_map/ppermute | solution.py:405
  21.4 4.4 %inner_lines.1 = (f32[16,6,128]{2,1,0:T(8,128)S(1)}, f32[2,6,32,128]{3,2,1,0:T(8,128)S(1)}, f32[6,72,128]{2,1,0:T(8,128)S(1)}, f32[72,128]{1,0:T(8,128)S(1)}, f3...) custom-call(f32[288,128]{1,0:T(8,128)S(1)} %get-tuple-element.29.matrice, ...), custom_call_target="tpu_custom_call" | custom-call | flops 10000000000 | bytes 3000000 | tf_op jit(solution)/shard_map/inner_lines/pallas_call | solution.py:471
  25.8 0.0 collective-permute-done.2.y_odd
  25.9 0.0 collective-permute-done.3.y_even
  25.9 0.0 collective-permute-done.x_odd
  25.9 0.0 collective-permute-done.1.x_even
  25.9 4.2 %rim_lines.1 = (f32[16,6,128]{2,1,0:T(8,128)S(1)}, f32[6,72,128]{2,1,0:T(8,128)S(1)}) custom-call(f32[288,128]{1,0:T(8,128)S(1)} %get-tuple-element.29.matrices, f32[6,32,128]{2,1,0:T(8,128)S(1)} %collective-permute-done.x_odd, f32[6,32,128]{2,1,0:T(8,128)S(1)} %collective-permute-done.1.x_even, f32[6,4,128]{2,1,0:T(4,128)S(1)} %collective-permute-done.2.y_odd, ...), custom_call_target="tpu_custom_call" | custom-call | tf_op jit(solution)/shard_map/rim_lines/pallas_call | solution.py:500
  30.1 14.3 %all_to_all.5.incoming = f32[16,6,128]{2,1,0:T(8,128)S(1)} all-to-all(f32[16,6,128]{2,1,0:T(8,128)S(1)} %get-tuple-element.47), channel_id=1, replica_groups=mesh['blk'=16,'bal'=32] {'blk'}, dimensions={0} | all-to-all | bytes 98304 | tf_op jit(solution)/shard_map/all_to_all | solution.py:517
  44.4 1.7 %place_receptors.1 = f32[4,6,32,128]{3,2,1,0:T(8,128)} custom-call(f32[16,6,128]{2,1,0:T(8,128)S(1)} %all_to_all.5.incoming, f32[2,6,32,128]{3,2,1,0:T(8,128)S(1)} %get-tuple-element.48.near, f32[6,72,128]{2,1,0:T(8,128)S(1)} %get-tuple-element.49.rim, bf16[64,2048]{1,0:T(8,128)(2,1)S(1)} %get-tuple-element.50.lines, ...), custom_call_target="tpu_custom_call" | custom-call | tf_op jit(solution)/shard_map/place_receptors/pallas_call | solution.py:518
Async XLA Ops:
  2.6 23.3 %collective-permute-start.2 = (f32[6,4,128]{2,1,0:T(4,128)S(1)}, f32[6,4,128]{2,1,0:T(4,128)S(1)}, u32[]{:S(2)}, u32[]{:S(2)}) collective-permute-start(f32[6,4,128]{2,1,0:T(4,128)S(1)} %get-tuple-element.32), channel_id=1, source_target_pairs={{1,2},{3,4},{5,6},{7,8},{9,10},{11,12},{13,14},{15,16},{17,18},{19... | collective-permute-start | bytes 36872 | tf_op jit(solution)/shard_map/ppermute | solution.py:405
  13.5 12.4 %collective-permute-start.3 = (f32[6,4,128]{2,1,0:T(4,128)S(1)}, f32[6,4,128]{2,1,0:T(4,128)S(1)}, u32[]{:S(2)}, u32[]{:S(2)}) collective-permute-start(f32[6,4,128]{2,1,0:T(4,128)S(1)} %get-tuple-element.33), channel_id=1, source_target_pairs={{0,1},{2,3},{4,5},{6,7},{8,9},{10,11},{12,13},{14,15},{16,17},{18,... | collective-permute-start | bytes 36872 | tf_op jit(solution)/shard_map/ppermute | solution.py:405
  15.4 10.4 %collective-permute-start = (f32[6,32,128]{2,1,0:T(8,128)S(1)}, f32[6,32,128]{2,1,0:T(8,128)S(1)}, u32[]{:S(2)}, u32[]{:S(2)}) collective-permute-start(f32[6,32,128]{2,1,0:T(8,128)S(1)} %get-tuple-element.30), channel_id=1, source_target_pairs={{32,64},{96,128},{160,192},{224,256},{288,320},{352,384},{416,448}... | collective-permute-start | bytes 294920 | tf_op jit(solution)/shard_map/ppermute | solution.py:405
  19.5 6.4 %collective-permute-start.1 = (f32[6,32,128]{2,1,0:T(8,128)S(1)}, f32[6,32,128]{2,1,0:T(8,128)S(1)}, u32[]{:S(2)}, u32[]{:S(2)}) collective-permute-start(f32[6,32,128]{2,1,0:T(8,128)S(1)} %get-tuple-element.31), channel_id=1, source_target_pairs={{0,32},{64,96},{128,160},{192,224},{256,288},{320,352},{384,416},{... | collective-permute-start | bytes 294920 | tf_op jit(solution)/shard_map/ppermute | solution.py:405
